TPU v7x, 128 devices: a whole 4x4x4 slice. The times are simulated.
128 devices in a mesh: clip: 32 (over y, x_hi, z), ha: 4 (over x_lo, core).
Axes of the slice: x: 4 (x_hi: 2, x_lo: 2; x = x_hi * 2 + x_lo), y: 4, z: 4, core: 2. Of those that a mesh axis runs over, the one named last changes fastest.
Arguments:
- frames: bfloat16 [120, 64, 32, 256], P(None, 'clip', 'ha'), may hold values from -6 to 6
- ln_gain: float32 [120], replicated, may hold values from 0.25 to 1.75
- w_qkv: bfloat16 [360, 120], replicated, may hold values from -4 to 4
- w_proj: bfloat16 [120, 240], replicated, may hold values from -0.375 to 0.375
- conv_weight: bfloat16 [2, 3, 3, 120, 120], replicated, may hold values from -0.1875 to 0.1875
Outputs:
- restored: bfloat16 [120, 64, 32, 256], P(None, 'clip', 'ha')
All inputs are finite; a program needn't handle non-finite values.
Results may differ from a plain program's by a relative error of at most 0.012.
The roundings to bfloat16 on the way count: a program that leaves them out, or rounds other values in their place, can miss the bound.
Values may be sent and summed in bfloat16 or wider, within the bound.
A program may use at most 128 MiB of HBM per device.

v0:
```python
import jax
import jax.numpy as jnp
from jax import lax
from jax.sharding import PartitionSpec as P

HEADS = 6
WIN = 8


def extended(cells, sides, width):
    for axis, dim in sides:
        count = lax.axis_size(axis)
        ends = count - 1
        head = lax.slice_in_dim(cells, 0, width, axis=dim)
        tail = lax.slice_in_dim(cells, cells.shape[dim] - width, cells.shape[dim], axis=dim)
        cells = jnp.concatenate(
            [
                lax.ppermute(tail, axis, [(i, (i + 1) % count) for i in range(ends)]),
                cells,
                lax.ppermute(head, axis, [((i + 1) % count, i) for i in range(ends)]),
            ],
            axis=dim,
        )
    return cells


def from_behind(value, axis, by):
    devices = lax.axis_size(axis)
    pairs = [(i, i + by) for i in range(devices) if 0 <= i + by < devices]
    return lax.ppermute(value, axis, pairs)


def layer_norm(frames, ln_gain):
    values = frames.astype(jnp.float32)
    average = jnp.mean(values, axis=0, keepdims=True)
    spread = jnp.mean((values - average) ** 2, axis=0, keepdims=True)
    normed = (values - average) * lax.rsqrt(spread + 1e-05) * ln_gain[:, None, None, None]
    return normed.astype(jnp.bfloat16)


def project(weight, field):
    return jnp.einsum("oi,ifhw->ofhw", weight, field, preferred_element_type=jnp.float32)


def to_windows(field, groups):
    c, f, h, w = field.shape
    d = c // (groups * HEADS)
    shaped = field.reshape(groups, HEADS, d, f // 2, 2, h // WIN, WIN, w // WIN, WIN)
    shaped = shaped.transpose(0, 1, 3, 5, 7, 2, 4, 6, 8)
    return shaped.reshape(groups, HEADS, f // 2 * (h // WIN) * (w // WIN), d, 2 * WIN * WIN)


def from_windows(blocks, f, h, w):
    groups, heads, count, d, tokens = blocks.shape
    shaped = blocks.reshape(groups, heads, f // 2, h // WIN, w // WIN, d, 2, WIN, WIN)
    shaped = shaped.transpose(0, 1, 5, 2, 6, 3, 7, 4, 8)
    return shaped.reshape(groups * heads * d, f, h, w)


def attend(queries, keys_all, values_all, usable):
    score_scale = queries.shape[-2] ** (-0.5)
    scores = (
        jnp.einsum("ndq,ndk->nqk", queries, keys_all, preferred_element_type=jnp.float32)
        * score_scale
    )
    scores = jnp.where(usable, scores, -1e30)
    peak = jnp.max(scores, axis=-1, keepdims=True)
    weights = jnp.exp(scores - peak)
    weights = (weights / jnp.sum(weights, axis=-1, keepdims=True)).astype(jnp.bfloat16)
    result = jnp.einsum("nqk,ndk->ndq", weights, values_all, preferred_element_type=jnp.float32)
    return result.astype(jnp.bfloat16)


def convolve(field, weight):
    rows_out = field.shape[2] - 2
    width = field.shape[3]
    padded = jnp.pad(field, ((0, 0), (0, 0), (0, 0), (1, 1)))
    total = jnp.zeros((weight.shape[2], field.shape[1], rows_out, width), jnp.float32)
    for row_off in range(3):
        for col_off in range(3):
            piece = padded[:, :, row_off : row_off + rows_out, col_off : col_off + width]
            total = total + jnp.einsum(
                "oi,ifhw->ofhw", weight[row_off, col_off], piece, preferred_element_type=jnp.float32
            )
    return total


def border_rows(field):
    return extended(field, (("ha", 2),), 1)


def shards(frames, ln_gain, w_qkv, w_proj, conv_weight):
    c, f, h, w = frames.shape
    normed = layer_norm(frames, ln_gain)
    projected = project(w_qkv, normed).astype(jnp.bfloat16)
    kv_before = from_behind(projected[c:], "clip", 1)
    kv_following = from_behind(projected[c:], "clip", -1)
    clip_index = lax.axis_index("clip")
    clip_count = lax.axis_size("clip")
    tokens_win = 2 * WIN * WIN
    usable_self = jnp.ones((tokens_win,), bool)
    usable_mut = jnp.concatenate(
        [
            jnp.broadcast_to(clip_index > 0, (tokens_win,)),
            jnp.broadcast_to(clip_index < clip_count - 1, (tokens_win,)),
        ]
    )
    own_win = to_windows(projected, 3)
    before_win = to_windows(kv_before, 2)
    later_win = to_windows(kv_following, 2)

    def per_head(members):
        own_head, before_head, later_head = members
        self_part = attend(own_head[0], own_head[1], own_head[2], usable_self)
        keys_both = jnp.concatenate([before_head[0], later_head[0]], axis=-1)
        values_both = jnp.concatenate([before_head[1], later_head[1]], axis=-1)
        mutual_part = attend(own_head[0], keys_both, values_both, usable_mut)
        return jnp.stack([self_part, mutual_part], axis=0)

    head_results = lax.map(
        per_head,
        (
            own_win.transpose(1, 0, 2, 3, 4),
            before_win.transpose(1, 0, 2, 3, 4),
            later_win.transpose(1, 0, 2, 3, 4),
        ),
    )
    joined = from_windows(head_results.transpose(1, 0, 2, 3, 4), f, h, w)
    attended = (frames.astype(jnp.float32) + project(w_proj, joined)).astype(jnp.bfloat16)
    inner_act = jnp.maximum(convolve(border_rows(attended), conv_weight[0]), 0.0).astype(
        jnp.bfloat16
    )
    branch = convolve(border_rows(inner_act), conv_weight[1])
    return (attended.astype(jnp.float32) + branch).astype(jnp.bfloat16)


def solution(mesh):
    return jax.shard_map(
        shards,
        mesh=mesh,
        in_specs=(P(None, "clip", "ha", None), P(), P(), P(), P()),
        out_specs=P(None, "clip", "ha", None),
        check_vma=False,
    )
```

profile of v0, /device:TPU:17, one launch (start us, length us, event | category | flops | bytes accessed | tf_op | source)
XLA Modules:
  0.0 374.9 jit_solution(271482495167527931)
XLA Ops:
  5.8 3.5 collective-permute-start
  9.3 6.4 %collective-permute-start.1 = (bf16[240,2,8,256]{3,0,2,1:T(8,128)(2,1)}, bf16[240,2,8,256]{3,0,2,1:T(8,128)(2,1)}, u32[]{:S(2)}, u32[]{:S(2)}) collective-permute-start(bf16[240,2,8,256]{3,0,2,1:T(8,128)(2,1)} %slice.206), channel_id=1, source_target_pairs={{4,0},{8,4},{12,8},{16,12},{20,16},{24,20},{28,24},{32,28},{36,32}... | collective-permute-start | bytes 5898248 | tf_op jit(solution)/shard_map/ppermute | solution.py:30
  18.5 25.1 %reshape.55 = bf16[3,6,20,1,2,1,8,32,8]{2,1,0,8,7,6,4,5,3:T(8,128)(2,1)} reshape(bf16[360,2,8,256]{0,3,2,1:T(8,128)(2,1)} %copy.15) | data formatting | bytes 5898240 | tf_op jit(solution)/shard_map/reshape | solution.py:48
  43.6 34.2 %copy.16 = bf16[3,6,1,1,32,20,2,8,8]{4,8,7,6,5,1,0,3,2:T(8,128)(2,1)} copy(bf16[3,6,1,1,32,20,2,8,8]{5,1,0,8,4,7,6,3,2:T(8,128)(2,1)} %bitcast.243) | data formatting | bytes 5898240 | tf_op jit(solution)/shard_map/transpose | solution.py:49
  77.8 14.6 %copy.21 = bf16[6,3,32,20,128]{4,3,2,1,0:T(8,128)(2,1)} copy(bf16[6,3,32,20,128]{2,4,3,0,1:T(8,128)(2,1)} %bitcast.246) | data formatting | bytes 5898240 | tf_op jit(solution)/shard_map/while | solution.py:120
  96.0 17.1 %reshape.57 = bf16[2,6,20,1,2,1,8,32,8]{2,1,0,8,7,6,4,5,3:T(8,128)(2,1)} reshape(bf16[240,2,8,256]{0,3,2,1:T(8,128)(2,1)S(1)} %copy.17) | data formatting | bytes 3932160 | tf_op jit(solution)/shard_map/reshape | solution.py:48
  113.1 23.4 %copy.18 = bf16[2,6,1,1,32,20,2,8,8]{4,8,7,6,5,1,0,3,2:T(8,128)(2,1)} copy(bf16[2,6,1,1,32,20,2,8,8]{5,1,0,8,4,7,6,3,2:T(8,128)(2,1)} %bitcast.244) | data formatting | bytes 3932160 | tf_op jit(solution)/shard_map/transpose | solution.py:49
  136.5 8.8 %copy.22 = bf16[6,2,32,20,128]{4,3,2,1,0:T(8,128)(2,1)} copy(bf16[6,2,32,20,128]{2,4,3,0,1:T(8,128)(2,1)} %bitcast.247) | data formatting | bytes 3932160 | tf_op jit(solution)/shard_map/while | solution.py:120
  148.1 17.1 %reshape.59 = bf16[2,6,20,1,2,1,8,32,8]{2,1,0,8,7,6,4,5,3:T(8,128)(2,1)} reshape(bf16[240,2,8,256]{0,3,2,1:T(8,128)(2,1)S(1)} %copy.19) | data formatting | bytes 3932160 | tf_op jit(solution)/shard_map/reshape | solution.py:48
  165.3 23.4 %copy.20 = bf16[2,6,1,1,32,20,2,8,8]{4,8,7,6,5,1,0,3,2:T(8,128)(2,1)} copy(bf16[2,6,1,1,32,20,2,8,8]{5,1,0,8,4,7,6,3,2:T(8,128)(2,1)} %bitcast.245) | data formatting | bytes 3932160 | tf_op jit(solution)/shard_map/transpose | solution.py:49
  188.6 7.8 %copy.23 = bf16[6,2,32,20,128]{4,3,2,1,0:T(8,128)(2,1)S(1)} copy(bf16[6,2,32,20,128]{2,4,3,0,1:T(8,128)(2,1)} %bitcast.248) | data formatting | bytes 3932160 | tf_op jit(solution)/shard_map/while | solution.py:120
  196.4 87.6 %while.10 = (s32[]{:T(128)}, bf16[6,2,32,20,128]{4,3,2,1,0:T(8,128)(2,1)}, bf16[6,3,32,20,128]{4,3,2,1,0:T(8,128)(2,1)}, bf16[6,2,32,20,128]{4,3,2,1,0:T(8,128)(...) while((s32[]{:T(128)}, ...), condition=%wide.region_7.8_spmd, body=%wide.region_2.7_spmd.sunk | while | flops 136872320 | bytes 16452493 | solution.py:120
  197.6 4.4 %fusion.125 = (f32[32,128]{1,0:T(8,128)S(1)}, f32[32,128,256]{2,1,0:T(8,128)}) fusion(pred[256]{0:T(512)(128)(4,1)S(1)} %get-tuple-element.150, bf16[32,20,128]{2,1,0:T(8,128)(2,1)S(1)} %get-tuple-element.117, bf16[32,20,128]{2,1,0:T(8,128)(2,1)S(1)} %get-tuple-element.118, bf16[6,3,32,20,128]{4,3,2,1,0:T(8,128)(2,1)} %get-tuple-element.147, ...), kind=kOutput, calls=%fused_computation.145.clone.1 | convolution fusion | flops 46792960 | bytes 4735744 | tf_op jit(solution)/shard_map/while/body/eval_jaxpr/sub | solution.py:68
  212.2 4.4 %fusion.125 = (f32[32,128]{1,0:T(8,128)S(1)}, f32[32,128,256]{2,1,0:T(8,128)}) fusion(pred[256]{0:T(512)(128)(4,1)S(1)} %get-tuple-element.150, bf16[32,20,128]{2,1,0:T(8,128)(2,1)S(1)} %get-tuple-element.117, bf16[32,20,128]{2,1,0:T(8,128)(2,1)S(1)} %get-tuple-element.118, bf16[6,3,32,20,128]{4,3,2,1,0:T(8,128)(2,1)} %get-tuple-element.147, ...), kind=kOutput, calls=%fused_computation.145.clone.1 | convolution fusion | flops 46792960 | bytes 4735744 | tf_op jit(solution)/shard_map/while/body/eval_jaxpr/sub | solution.py:68
  226.8 4.4 %fusion.125 = (f32[32,128]{1,0:T(8,128)S(1)}, f32[32,128,256]{2,1,0:T(8,128)}) fusion(pred[256]{0:T(512)(128)(4,1)S(1)} %get-tuple-element.150, bf16[32,20,128]{2,1,0:T(8,128)(2,1)S(1)} %get-tuple-element.117, bf16[32,20,128]{2,1,0:T(8,128)(2,1)S(1)} %get-tuple-element.118, bf16[6,3,32,20,128]{4,3,2,1,0:T(8,128)(2,1)} %get-tuple-element.147, ...), kind=kOutput, calls=%fused_computation.145.clone.1 | convolution fusion | flops 46792960 | bytes 4735744 | tf_op jit(solution)/shard_map/while/body/eval_jaxpr/sub | solution.py:68
  241.4 4.4 %fusion.125 = (f32[32,128]{1,0:T(8,128)S(1)}, f32[32,128,256]{2,1,0:T(8,128)}) fusion(pred[256]{0:T(512)(128)(4,1)S(1)} %get-tuple-element.150, bf16[32,20,128]{2,1,0:T(8,128)(2,1)S(1)} %get-tuple-element.117, bf16[32,20,128]{2,1,0:T(8,128)(2,1)S(1)} %get-tuple-element.118, bf16[6,3,32,20,128]{4,3,2,1,0:T(8,128)(2,1)} %get-tuple-element.147, ...), kind=kOutput, calls=%fused_computation.145.clone.1 | convolution fusion | flops 46792960 | bytes 4735744 | tf_op jit(solution)/shard_map/while/body/eval_jaxpr/sub | solution.py:68
  248.8 3.2 fusion.127
  256.0 4.4 %fusion.125 = (f32[32,128]{1,0:T(8,128)S(1)}, f32[32,128,256]{2,1,0:T(8,128)}) fusion(pred[256]{0:T(512)(128)(4,1)S(1)} %get-tuple-element.150, bf16[32,20,128]{2,1,0:T(8,128)(2,1)S(1)} %get-tuple-element.117, bf16[32,20,128]{2,1,0:T(8,128)(2,1)S(1)} %get-tuple-element.118, bf16[6,3,32,20,128]{4,3,2,1,0:T(8,128)(2,1)} %get-tuple-element.147, ...), kind=kOutput, calls=%fused_computation.145.clone.1 | convolution fusion | flops 46792960 | bytes 4735744 | tf_op jit(solution)/shard_map/while/body/eval_jaxpr/sub | solution.py:68
  270.6 4.4 %fusion.125 = (f32[32,128]{1,0:T(8,128)S(1)}, f32[32,128,256]{2,1,0:T(8,128)}) fusion(pred[256]{0:T(512)(128)(4,1)S(1)} %get-tuple-element.150, bf16[32,20,128]{2,1,0:T(8,128)(2,1)S(1)} %get-tuple-element.117, bf16[32,20,128]{2,1,0:T(8,128)(2,1)S(1)} %get-tuple-element.118, bf16[6,3,32,20,128]{4,3,2,1,0:T(8,128)(2,1)} %get-tuple-element.147, ...), kind=kOutput, calls=%fused_computation.145.clone.1 | convolution fusion | flops 46792960 | bytes 4735744 | tf_op jit(solution)/shard_map/while/body/eval_jaxpr/sub | solution.py:68
  284.1 8.4 %copy.24 = bf16[6,2,32,20,128]{2,4,3,0,1:T(8,128)(2,1)} copy(bf16[6,2,32,20,128]{4,3,2,1,0:T(8,128)(2,1)} %get-tuple-element.37) | data formatting | bytes 3932160 | tf_op jit(solution)/shard_map/while | solution.py:120
  292.5 31.2 %copy.25 = bf16[2,6,20,1,2,1,8,32,8]{2,1,0,8,7,6,4,5,3:T(8,128)(2,1)} copy(bf16[2,6,20,1,2,1,8,32,8]{7,8,6,4,2,1,0,5,3:T(8,128)(2,1)} %bitcast.249) | data formatting | bytes 3932160 | tf_op jit(solution)/shard_map/transpose | solution.py:56
  323.7 18.9 %reshape.62 = bf16[240,2,8,256]{0,3,2,1:T(8,128)(2,1)S(1)} reshape(bf16[2,6,20,1,2,1,8,32,8]{2,1,0,8,7,6,4,5,3:T(8,128)(2,1)} %copy.25) | data formatting | bytes 3932160 | tf_op jit(solution)/shard_map/reshape | solution.py:57
  343.5 4.1 %collective-permute-start.2 = (bf16[120,2,1,256]{3,0,2,1:T(8,128)(2,1)S(1)}, bf16[120,2,1,256]{3,0,2,1:T(8,128)(2,1)S(1)}, u32[]{:S(2)}, u32[]{:S(2)}) collective-permute-start(bf16[120,2,1,256]{3,0,2,1:T(8,128)(2,1)S(1)} %get-tuple-element.68), channel_id=1, source_target_pairs={{0,1},{1,2},{2,3},{4,5},{5,6},{6,7},{8,9},{9,10},{10,11},{12,13},{... | collective-permute-start | bytes 368648 | tf_op jit(solution)/shard_map/ppermute | solution.py:18
  350.0 3.8 %collective-permute-done.3 = bf16[120,2,1,256]{3,0,2,1:T(8,128)(2,1)S(1)} collective-permute-done((bf16[120,2,1,256]{3,0,2,1:T(8,128)(2,1)S(1)}, bf16[120,2,1,256]{3,0,2,1:T(8,128)(2,1)S(1)}, u32[]{:S(2)}, u32[]{:S(2)}) %collective-permute-start.3) | collective-permute-done | bytes 122912 | tf_op jit(solution)/shard_map/ppermute | solution.py:20
  (90 shorter events, 96.9 us)
Async XLA Ops:
  0.0 3.2 copy-start
  0.0 3.2 copy-start.2
  0.0 3.2 copy-start.7
  5.8 87.4 %collective-permute-start = (bf16[240,2,8,256]{3,0,2,1:T(8,128)(2,1)}, bf16[240,2,8,256]{3,0,2,1:T(8,128)(2,1)}, u32[]{:S(2)}, u32[]{:S(2)}) collective-permute-start(bf16[240,2,8,256]{3,0,2,1:T(8,128)(2,1)} %slice.206), channel_id=1, source_target_pairs={{0,4},{4,8},{8,12},{12,16},{16,20},{20,24},{24,28},{28,32},{32,36}... | collective-permute-start | bytes 5898248 | tf_op jit(solution)/shard_map/ppermute | solution.py:30
  9.3 136.0 %collective-permute-start.1 = (bf16[240,2,8,256]{3,0,2,1:T(8,128)(2,1)}, bf16[240,2,8,256]{3,0,2,1:T(8,128)(2,1)}, u32[]{:S(2)}, u32[]{:S(2)}) collective-permute-start(bf16[240,2,8,256]{3,0,2,1:T(8,128)(2,1)} %slice.206), channel_id=1, source_target_pairs={{4,0},{8,4},{12,8},{16,12},{20,16},{24,20},{28,24},{32,28},{36,32}... | collective-permute-start | bytes 5898248 | tf_op jit(solution)/shard_map/ppermute | solution.py:30
  77.8 14.6 %copy-start.5 = (bf16[2,3,3,120,120]{4,3,2,1,0:T(8,128)(2,1)S(1)}, bf16[2,3,3,120,120]{4,3,2,1,0:T(8,128)(2,1)}, u32[]{:S(2)}) copy-start(bf16[2,3,3,120,120]{4,3,2,1,0:T(8,128)(2,1)} %param.11) | copy-start | bytes 1555204
  323.7 18.9 %copy-start.3 = (bf16[120,2,8,256]{3,2,1,0:T(8,128)(2,1)S(1)}, bf16[120,2,8,256]{3,2,1,0:T(8,128)(2,1)}, u32[]{:S(2)}) copy-start(bf16[120,2,8,256]{3,2,1,0:T(8,128)(2,1)} %param.7) | copy-start | bytes 2949124
  323.7 18.9 %copy-start.6 = (bf16[120,240]{1,0:T(8,128)(2,1)S(1)}, bf16[120,240]{1,0:T(8,128)(2,1)}, u32[]{:S(2)}) copy-start(bf16[120,240]{1,0:T(8,128)(2,1)} %param.10) | copy-start | bytes 172804
  342.6 6.9 %copy-start.4 = (bf16[3,3,120,120]{3,2,1,0:T(8,128)(2,1)S(1)}, bf16[3,3,120,120]{3,2,1,0:T(8,128)(2,1)}, u32[]{:S(2)}) copy-start(bf16[3,3,120,120]{3,2,1,0:T(8,128)(2,1)} %get-tuple-element.71) | copy-start | bytes 777604
  343.5 6.5 %collective-permute-start.2 = (bf16[120,2,1,256]{3,0,2,1:T(8,128)(2,1)S(1)}, bf16[120,2,1,256]{3,0,2,1:T(8,128)(2,1)S(1)}, u32[]{:S(2)}, u32[]{:S(2)}) collective-permute-start(bf16[120,2,1,256]{3,0,2,1:T(8,128)(2,1)S(1)} %get-tuple-element.68), channel_id=1, source_target_pairs={{0,1},{1,2},{2,3},{4,5},{5,6},{6,7},{8,9},{9,10},{10,11},{12,13},{... | collective-permute-start | bytes 368648 | tf_op jit(solution)/shard_map/ppermute | solution.py:18
  347.6 6.2 %collective-permute-start.3 = (bf16[120,2,1,256]{3,0,2,1:T(8,128)(2,1)S(1)}, bf16[120,2,1,256]{3,0,2,1:T(8,128)(2,1)S(1)}, u32[]{:S(2)}, u32[]{:S(2)}) collective-permute-start(bf16[120,2,1,256]{3,0,2,1:T(8,128)(2,1)S(1)} %get-tuple-element.69), channel_id=1, source_target_pairs={{1,0},{2,1},{3,2},{5,4},{6,5},{7,6},{9,8},{10,9},{11,10},{13,12},{... | collective-permute-start | bytes 368648 | tf_op jit(solution)/shard_map/ppermute | solution.py:20
  359.7 5.0 %collective-permute-start.4 = (bf16[120,2,1,256]{3,0,2,1:T(8,128)(2,1)S(1)}, bf16[120,2,1,256]{3,0,2,1:T(8,128)(2,1)S(1)}, u32[]{:S(2)}, u32[]{:S(2)}) collective-permute-start(bf16[120,2,1,256]{3,0,2,1:T(8,128)(2,1)S(1)} %get-tuple-element.66), channel_id=1, source_target_pairs={{0,1},{1,2},{2,3},{4,5},{5,6},{6,7},{8,9},{9,10},{10,11},{12,13},{... | collective-permute-start | bytes 368648 | tf_op jit(solution)/shard_map/ppermute | solution.py:18
  361.6 6.2 %collective-permute-start.5 = (bf16[120,2,1,256]{3,0,2,1:T(8,128)(2,1)S(1)}, bf16[120,2,1,256]{3,0,2,1:T(8,128)(2,1)S(1)}, u32[]{:S(2)}, u32[]{:S(2)}) collective-permute-start(bf16[120,2,1,256]{3,0,2,1:T(8,128)(2,1)S(1)} %get-tuple-element.67), channel_id=1, source_target_pairs={{1,0},{2,1},{3,2},{5,4},{6,5},{7,6},{9,8},{10,9},{11,10},{13,12},{... | collective-permute-start | bytes 368648 | tf_op jit(solution)/shard_map/ppermute | solution.py:20
  372.1 2.8 copy-start.1
where the time goes:
time: 380 us; the launch traced here: 375 us
  local copies, waits for them, and re-layouts  249 us (66%)
  matrix products  88.2 us (23%)
  starting transfers between devices  20.5 us (5%)
  other arithmetic  10.2 us (3%)
  waiting for transfers between devices  6.99 us (2%)
    transpose x3, local copies, waits for them, and re-layouts, to_windows(): shaped = shaped.transpose(0, 1, 3, 5, 7, 2, 4, 6, 8)  80.9 us
    reshape x3, local copies, waits for them, and re-layouts, to_windows(): field.reshape(groups, HEADS, d, f // 2, 2, h // WIN, WIN, w // WIN, WIN)  59.3 us
    sub x12, matrix products, attend(): weights = jnp.exp(scores - peak)  45.8 us
    while x4, local copies, waits for them, and re-layouts, shards(): lax.map(per_head, (own_win.transpose(1, 0, 2, 3, 4), before_win.transpose...  39.6 us
    transpose x1, local copies, waits for them, and re-layouts, from_windows(): shaped = shaped.transpose(0, 1, 5, 2, 6, 3, 7, 4, 8)  31.2 us
    dot_general x12, matrix products, attend(): jnp.einsum('nqk,ndk->ndq', weights, values_all, preferred_element_type=jn...  30.2 us
    reshape x1, local copies, waits for them, and re-layouts, from_windows(): return shaped.reshape(groups * heads * d, f, h, w)  18.9 us
    dot_general x18, matrix products, convolve(): jnp.einsum('oi,ifhw->ofhw', weight[row_off, col_off], piece, preferred_el...  10.3 us
  transfers between devices with their start and end apart: 6, of which 2 were waited for; matrix products, arithmetic and copies ran while one was open for 35% of the time, Pallas kernels for 0%

commit v1 on v0

v1 whole, which is shorter than its diff:
```python
import functools
import math

import jax
import jax.numpy as jnp
from jax import lax
from jax.experimental import pallas as pl
from jax.experimental.pallas import tpu as pltpu
from jax.sharding import PartitionSpec as P

HEADS = 6
WIN = 8
C = 120
D = C // HEADS
CP = 128
DP = 32
TOK = 2 * WIN * WIN
CHUNKS = 4
HALO = 2
MESH = pl.DeviceIdType.MESH
F32 = jnp.float32
BF16 = jnp.bfloat16


def dot(a, b):
    return lax.dot_general(a, b, (((1,), (0,)), ((), ())), preferred_element_type=F32)


def dot_nt(a, b):
    return lax.dot_general(a, b, (((1,), (1,)), ((), ())), preferred_element_type=F32)


def iota(shape, dim):
    return lax.broadcasted_iota(jnp.int32, shape, dim)


def one_hot_heads(rows, cols, padded_dim):
    padded = iota((rows, cols), padded_dim)
    packed = iota((rows, cols), 1 - padded_dim)
    entry = padded & (DP - 1)
    hit = ((padded >> 5) * D + entry == packed) & (entry < D)
    return jnp.where(hit, 1.0, 0.0).astype(BF16)


def pad_rows(value, rows):
    extra = jnp.zeros((rows - value.shape[0], value.shape[1]), value.dtype)
    return jnp.concatenate([value, extra], axis=0)


def kernel(
    clips,
    parts,
    x_ref,
    gain_ref,
    wqkv_ref,
    wproj_ref,
    wconv_ref,
    out_ref,
    xn,
    xin,
    q_s,
    k_s,
    v_s,
    k2_s,
    v2_s,
    o_s,
    att,
    inner,
    wq_s,
    wk_s,
    wv_s,
    wp_s,
    wc_s,
    mask_s,
    left_s,
    right_s,
    send_sem,
    recv_sem,
    hsend_sem,
    hrecv_sem,
):
    me = lax.axis_index("clip")
    ha = lax.axis_index("ha")
    windows = x_ref.shape[0]
    per = windows // CHUNKS
    width = windows * WIN
    has_prev, has_next = me > 0, me < clips - 1
    has_up, has_down = ha > 0, ha < parts - 1

    att[...] = jnp.zeros_like(att)
    lane_one = jnp.where(iota((TOK, CP), 1) == C, 1.0, 0.0).astype(BF16)

    barrier = pltpu.get_barrier_semaphore()
    neighbours = (
        (has_prev, (me - 1, ha)),
        (has_next, (me + 1, ha)),
        (has_up, (me, ha - 1)),
        (has_down, (me, ha + 1)),
    )
    for there, device in neighbours:

        @pl.when(there)
        def _(device=device):
            pl.semaphore_signal(barrier, inc=1, device_id=device, device_id_type=MESH)

    wqkv = wqkv_ref[...].astype(F32)
    for slot, start in ((wq_s, 0), (wk_s, C)):
        slot[...] = jnp.zeros_like(slot)
        slot[:, :C] = pad_rows(wqkv[start : start + C], CP).astype(BF16)
    wv = dot(one_hot_heads(HEADS * DP, C, 0), wqkv[2 * C :].astype(BF16))
    ones_row = (iota((HEADS * DP, CP), 0) & (DP - 1) == D) & (iota((HEADS * DP, CP), 1) == C)
    wv_s[...] = jnp.where(ones_row, 1.0, 0.0).astype(BF16)
    wv_s[:, :C] = wv.astype(BF16)
    wp = dot(wproj_ref[...], one_hot_heads(2 * C, 2 * HEADS * DP, 1))
    wp_s[...] = pad_rows(wp, CP).astype(BF16)
    channel = iota((CP, TOK), 0)
    for h in range(HEADS):
        mask_s[h] = jnp.where((channel >= h * D) & (channel < (h + 1) * D), 1.0, 0.0).astype(BF16)

    gain = gain_ref[...]

    def norm_window(w, carry):
        x = x_ref[w].astype(F32)
        centred = x - jnp.mean(x, axis=-1, keepdims=True)
        spread = jnp.mean(centred * centred, axis=-1, keepdims=True)
        normed = centred * lax.rsqrt(spread + 1e-05) * gain
        xn[w] = lane_one
        xn[w, :, :C] = normed.astype(BF16)
        return carry

    def clip_copy(side, k):
        part = pl.ds(k * per, per)
        return pltpu.make_async_remote_copy(
            src_ref=xn.at[part],
            dst_ref=xin.at[side, part],
            send_sem=send_sem.at[side, k],
            recv_sem=recv_sem.at[side, k],
            device_id=(me + 1 - 2 * side, ha),
            device_id_type=MESH,
        )

    for k in range(CHUNKS):
        lax.fori_loop(k * per, (k + 1) * per, norm_window, 0, unroll=4)
        if k == 0:
            pl.semaphore_wait(barrier, sum(jnp.where(there, 1, 0) for there, _ in neighbours))

        @pl.when(has_next)
        def _(k=k):
            clip_copy(0, k).start()

        @pl.when(has_prev)
        def _(k=k):
            clip_copy(1, k).start()

    scale = math.log2(math.e) / math.sqrt(D)

    def attend(w, keys, values, first_row):
        q = q_s[w]
        for pair in range(HEADS // 2):
            queries = jnp.concatenate([q * mask_s[2 * pair], q * mask_s[2 * pair + 1]], axis=1)
            scores = dot(keys, queries)
            peak = jnp.max(scores, axis=0, keepdims=True)
            weights = jnp.exp2((scores - peak) * scale).astype(BF16)
            rows = pl.ds(2 * pair * DP, 2 * DP)
            got = dot(values[2 * pair * DP : 2 * (pair + 1) * DP], weights)
            for side in range(2):
                mine = got[side * DP : (side + 1) * DP, side * TOK : (side + 1) * TOK]
                mine = mine * (1.0 / mine[D : D + 1])
                start = first_row + (2 * pair + side) * DP
                o_s[w, start : start + DP] = mine.astype(BF16)

    def project_own(w, carry):
        x = xn[w]
        q_s[w] = dot_nt(wq_s[...], x).astype(BF16)
        k_s[w] = dot_nt(x, wk_s[...]).astype(BF16)
        v_s[w] = dot_nt(wv_s[...], x).astype(BF16)
        return carry

    lax.fori_loop(0, windows, project_own, 0, unroll=4)

    def self_window(w, carry):
        attend(w, k_s[w], v_s[w], 0)
        return carry

    lax.fori_loop(0, windows, self_window, 0, unroll=2)

    wc_s[...] = jnp.zeros_like(wc_s)
    for layer in range(2):
        for r in range(3):
            for s in range(3):
                weight = pad_rows(wconv_ref[layer, r, s].astype(F32), CP).astype(BF16)
                wc_s[layer, s * CP : (s + 1) * CP, r * CP : r * CP + C] = weight
    left_s[...] = jnp.zeros_like(left_s)
    right_s[...] = jnp.zeros_like(right_s)

    slot_prev = jnp.where(has_prev, 0, 1)
    slot_next = jnp.where(has_next, 1, 0)
    own_rows = x_ref.shape[1] // (2 * WIN)

    def project_both(w, carry):
        x = jnp.concatenate([xin[slot_prev, w], xin[slot_next, w]], axis=0)
        k2_s[w] = dot_nt(x, wk_s[...]).astype(BF16)
        v2_s[w] = dot_nt(wv_s[...], x).astype(BF16)
        return carry

    def mutual_window(w, carry):
        attend(w, k2_s[w], v2_s[w], HEADS * DP)
        return carry

    def finish_pair(p, carry):
        both = []
        for side in range(2):
            w = 2 * p + side
            mixed = dot(wp_s[...], o_s[w]).T
            both.append(x_ref[w].astype(F32) + mixed[:, :C])
        shaped = jnp.stack(both, axis=0).reshape(2, 2, own_rows, WIN, C)
        shaped = shaped.transpose(1, 2, 0, 3, 4).reshape(2, own_rows, 2 * WIN, C)
        cols = pl.ds(pl.multiple_of(p * 2 * WIN, 2 * WIN), 2 * WIN)
        att[:, HALO : HALO + own_rows, cols, :C] = shaped.astype(BF16)
        return carry

    def halo_copy(side, k):
        cols = pl.ds(k * per * WIN, per * WIN)
        src_row = own_rows if side else HALO
        dst_row = 0 if side else HALO + own_rows
        return pltpu.make_async_remote_copy(
            src_ref=att.at[:, pl.ds(src_row, HALO), cols],
            dst_ref=att.at[:, pl.ds(dst_row, HALO), cols],
            send_sem=hsend_sem.at[side, k],
            recv_sem=hrecv_sem.at[side, k],
            device_id=(me, ha + (1 if side else -1)),
            device_id_type=MESH,
        )

    for k in range(CHUNKS):

        @pl.when(has_prev)
        def _(k=k):
            clip_copy(0, k).wait_recv()

        @pl.when(has_next)
        def _(k=k):
            clip_copy(1, k).wait_recv()

        lax.fori_loop(k * per, (k + 1) * per, project_both, 0, unroll=4)
        lax.fori_loop(k * per, (k + 1) * per, mutual_window, 0, unroll=2)
        lax.fori_loop(k * per // 2, (k + 1) * per // 2, finish_pair, 0, unroll=2)

        @pl.when(has_up)
        def _(k=k):
            halo_copy(0, k).start()

        @pl.when(has_down)
        def _(k=k):
            halo_copy(1, k).start()

    def convolve(field, row, layer, f):
        stacked = jnp.concatenate([field[f, row], field[f, row + 1], field[f, row + 2]], axis=1)
        part = dot_nt(stacked, wc_s[layer])
        left_s[f, 8 : 8 + width] = part[:, :CP]
        right_s[f, 0:width] = part[:, 2 * CP :]
        return part[:, CP : 2 * CP] + left_s[f, 7 : 7 + width] + right_s[f, 1 : 1 + width]

    def first_conv(row, carry):
        for f in range(2):
            inner[f, row] = jnp.maximum(convolve(att, row, 0, f), 0.0).astype(BF16)
        return carry

    def second_conv(row, carry):
        for f in range(2):
            total = att[f, row + HALO].astype(F32) + convolve(inner, row, 1, f)
            out_ref[f, row] = total[:, :C].astype(BF16)
        return carry

    lax.fori_loop(HALO, own_rows, first_conv, 0)
    for k in range(CHUNKS):

        @pl.when(has_down)
        def _(k=k):
            halo_copy(0, k).wait_recv()

        @pl.when(has_up)
        def _(k=k):
            halo_copy(1, k).wait_recv()

    lax.fori_loop(0, HALO, first_conv, 0)
    lax.fori_loop(own_rows, own_rows + HALO, first_conv, 0)

    @pl.when(jnp.logical_not(has_up))
    def _():
        inner[:, 0] = jnp.zeros_like(inner[:, 0])

    @pl.when(jnp.logical_not(has_down))
    def _():
        inner[:, own_rows + 1] = jnp.zeros_like(inner[:, 0])

    lax.fori_loop(0, own_rows, second_conv, 0)

    for k in range(CHUNKS):
        for copy, low, high in ((clip_copy, has_next, has_prev), (halo_copy, has_up, has_down)):

            @pl.when(low)
            def _(copy=copy, k=k):
                copy(0, k).wait_send()

            @pl.when(high)
            def _(copy=copy, k=k):
                copy(1, k).wait_send()


def shards(frames, ln_gain, w_qkv, w_proj, conv_weight):
    c, f, h, w = frames.shape
    windows = w // WIN
    clips, parts = lax.axis_size("clip"), lax.axis_size("ha")
    tokens = frames.reshape(c, f, h, windows, WIN).transpose(3, 1, 2, 4, 0)
    tokens = tokens.reshape(windows, f * h * WIN, c)
    vmem = pl.BlockSpec(memory_space=pltpu.VMEM)
    restored = pl.pallas_call(
        functools.partial(kernel, clips, parts),
        out_shape=jax.ShapeDtypeStruct((f, h, w, c), BF16),
        in_specs=[vmem] * 5,
        out_specs=vmem,
        scratch_shapes=[
            pltpu.VMEM((windows, TOK, CP), BF16),
            pltpu.VMEM((2, windows, TOK, CP), BF16),
            pltpu.VMEM((windows, CP, TOK), BF16),
            pltpu.VMEM((windows, TOK, CP), BF16),
            pltpu.VMEM((windows, HEADS * DP, TOK), BF16),
            pltpu.VMEM((windows, 2 * TOK, CP), BF16),
            pltpu.VMEM((windows, HEADS * DP, 2 * TOK), BF16),
            pltpu.VMEM((windows, 2 * HEADS * DP, TOK), BF16),
            pltpu.VMEM((f, h + 2 * HALO, w, CP), BF16),
            pltpu.VMEM((f, h + 2, w, CP), BF16),
            pltpu.VMEM((CP, CP), BF16),
            pltpu.VMEM((CP, CP), BF16),
            pltpu.VMEM((HEADS * DP, CP), BF16),
            pltpu.VMEM((CP, 2 * HEADS * DP), BF16),
            pltpu.VMEM((2, 3 * CP, 3 * CP), BF16),
            pltpu.VMEM((HEADS, CP, TOK), BF16),
            pltpu.VMEM((f, w + 16, CP), F32),
            pltpu.VMEM((f, w + 16, CP), F32),
            pltpu.SemaphoreType.DMA((2, CHUNKS)),
            pltpu.SemaphoreType.DMA((2, CHUNKS)),
            pltpu.SemaphoreType.DMA((2, CHUNKS)),
            pltpu.SemaphoreType.DMA((2, CHUNKS)),
        ],
        compiler_params=pltpu.CompilerParams(
            collective_id=0, has_side_effects=True, vmem_limit_bytes=48 * 1024 * 1024
        ),
    )(tokens, ln_gain.reshape(1, c), w_qkv, w_proj, conv_weight)
    return restored.transpose(3, 0, 1, 2)


def solution(mesh):
    return jax.shard_map(
        shards,
        mesh=mesh,
        in_specs=(P(None, "clip", "ha", None), P(), P(), P(), P()),
        out_specs=P(None, "clip", "ha", None),
        check_vma=False,
    )
```

time: 380 us -> 78.9 us (0.21); the launches traced: 375 us -> 78.5 us
  local copies, waits for them, and re-layouts: 249 us -> 4.55 us
  matrix products: 88.2 us -> 0 us
  Pallas kernels: 0 us -> 73.9 us
  starting transfers between devices: 20.5 us -> 0 us
  other arithmetic: 10.2 us -> 0 us
  waiting for transfers between devices: 6.99 us -> 0 us
    transpose x4 -> x2, local copies, waits for them, and re-layouts: 112 us -> 1.93 us  [the longest x1 1.64 us: shards(): return restored.transpose(3, 0, 1, 2)]
    reshape x4 -> x0, local copies, waits for them, and re-layouts: 78.3 us -> none  [the longest x3 59.3 us: to_windows(): field.reshape(groups, HEADS, d, f // 2, 2, h // WIN, WIN, w // WIN, WIN)]
    pallas_call x0 -> x1, Pallas kernels: none -> 73.9 us  [shards(): pl.pallas_call(functools.partial(kernel, clips, parts), out_shape=jax.Sha...]
    sub x12 -> x0, matrix products: 45.8 us -> none  [attend(): weights = jnp.exp(scores - peak)]
    dot_general x32 -> x0, matrix products: 42.4 us -> none  [the longest x12 30.2 us: attend(): jnp.einsum('nqk,ndk->ndq', weights, values_all, preferred_element_type=jn...]
    while x4 -> x0, local copies, waits for them, and re-layouts: 39.6 us -> none  [shards(): lax.map(per_head, (own_win.transpose(1, 0, 2, 3, 4), before_win.transpose...]
    ppermute x6 -> x0, starting transfers between devices: 20.5 us -> none  [the longest x2 9.92 us: from_behind(): return lax.ppermute(value, axis, pairs)]
    squeeze x7 -> x0, local copies, waits for them, and re-layouts: 7.5 us -> none  [the longest x6 6.75 us: per_head(): values_both = jnp.concatenate([before_head[1], later_head[1]], axis=-1)]
  transfers between devices with their start and end apart: 6 -> 0, of which waited for: 2 -> 0; matrix products, arithmetic and copies ran while one was open for 35% -> 0% of each run, Pallas kernels for 0% -> 0%
where the time goes in v1:
time: 78.9 us; the launch traced here: 78.5 us
  Pallas kernels  73.9 us (94%)
  local copies, waits for them, and re-layouts  4.55 us (6%)
    pallas_call x1, Pallas kernels, shards(): pl.pallas_call(functools.partial(kernel, clips, parts), out_shape=jax.Sha...  73.9 us
    unnamed x9, local copies, waits for them, and re-layouts  2.63 us
    transpose x1, local copies, waits for them, and re-layouts, shards(): return restored.transpose(3, 0, 1, 2)  1.64 us

profile of v1, /device:TPU:17, one launch (start us, length us, event | category | flops | bytes accessed | tf_op | source)
XLA Modules:
  0.0 78.5 jit_solution(8932981378534031808)
XLA Ops:
  0.0 1.9 %copy.8 = bf16[120,2,8,256]{0,3,2,1:T(8,128)(2,1)S(1)} copy(bf16[120,2,8,256]{3,2,1,0:T(8,128)(2,1)} %param.5) | data formatting | bytes 1966080 | tf_op args[0]
  1.9 0.0 copy-start
  1.9 0.0 copy-start.1
  1.9 0.0 copy-start.2
  1.9 0.3 copy.9
  2.2 0.0 copy-start.3
  2.2 0.7 copy-done
  3.0 0.0 copy-done.1
  3.0 0.0 copy-done.2
  3.0 0.0 copy-done.3
  3.0 73.9 %shard_map.55 = bf16[2,8,256,120]{3,2,1,0:T(8,128)(2,1)S(1)} custom-call(bf16[32,128,120]{2,1,0:T(8,128)(2,1)S(1)} %bitcast.6, f32[1,120]{1,0:T(1,128)S(1)} %bitcast.8, bf16[360,120]{1,0:T(8,128)(2,1)S(1)} %copy-done.1, bf16[120,240]{1,0:T(8,128)(2,1)S(1)} %copy-done.2, bf16[2,3,3,120,120]{4,3,2,1,0:T(8,128)(2,1)S(1)} %copy-done), custom_call_target="tpu_custom_call" | custom-call | tf_op jit(solution)/shard_map/pallas_call | solution.py:318
  76.9 1.6 %copy.10 = bf16[120,2,8,256]{3,2,1,0:T(8,128)(2,1)} copy(bf16[120,2,8,256]{0,3,2,1:T(8,128)(2,1)S(1)} %bitcast.7) | data formatting | bytes 1966080 | tf_op jit(solution)/shard_map/transpose | solution.py:351
Async XLA Ops:
  1.9 1.1 %copy-start = (bf16[2,3,3,120,120]{4,3,2,1,0:T(8,128)(2,1)S(1)}, bf16[2,3,3,120,120]{4,3,2,1,0:T(8,128)(2,1)}, u32[]{:S(2)}) copy-start(bf16[2,3,3,120,120]{4,3,2,1,0:T(8,128)(2,1)} %wconv_ref.1) | copy-start | bytes 1555204
  1.9 1.0 %copy-start.1 = (bf16[360,120]{1,0:T(8,128)(2,1)S(1)}, bf16[360,120]{1,0:T(8,128)(2,1)}, u32[]{:S(2)}) copy-start(bf16[360,120]{1,0:T(8,128)(2,1)} %wqkv_ref.1) | copy-start | bytes 259204
  1.9 1.0 %copy-start.2 = (bf16[120,240]{1,0:T(8,128)(2,1)S(1)}, bf16[120,240]{1,0:T(8,128)(2,1)}, u32[]{:S(2)}) copy-start(bf16[120,240]{1,0:T(8,128)(2,1)} %wproj_ref.1) | copy-start | bytes 172804
  2.2 0.7 copy-start.3

commit v2 on v1

--- a/solution.py
+++ b/solution.py
@@ -17,6 +17,10 @@
 TOK = 2 * WIN * WIN
 CHUNKS = 4
 HALO = 2
+GROUP = 4
+PROJ = 8
+FIN = 8
+ROWS = 2
 MESH = pl.DeviceIdType.MESH
 F32 = jnp.float32
 BF16 = jnp.bfloat16
@@ -154,35 +158,50 @@
 
     scale = math.log2(math.e) / math.sqrt(D)
 
-    def attend(w, keys, values, first_row):
-        q = q_s[w]
-        for pair in range(HEADS // 2):
-            queries = jnp.concatenate([q * mask_s[2 * pair], q * mask_s[2 * pair + 1]], axis=1)
-            scores = dot(keys, queries)
-            peak = jnp.max(scores, axis=0, keepdims=True)
-            weights = jnp.exp2((scores - peak) * scale).astype(BF16)
-            rows = pl.ds(2 * pair * DP, 2 * DP)
-            got = dot(values[2 * pair * DP : 2 * (pair + 1) * DP], weights)
+    def attend(ws, keys, values, first_row):
+        jobs = [(w, pair) for w in range(len(ws)) for pair in range(HEADS // 2)]
+        qs = [q_s[w] for w in ws]
+        scores = [
+            dot(
+                keys[w],
+                jnp.concatenate([qs[w] * mask_s[2 * pair], qs[w] * mask_s[2 * pair + 1]], axis=1),
+            )
+            for w, pair in jobs
+        ]
+        weights = []
+        for score in scores:
+            peak = jnp.max(score, axis=0, keepdims=True)
+            weights.append(jnp.exp2((score - peak) * scale).astype(BF16))
+        gots = [
+            dot(values[w][2 * pair * DP : 2 * (pair + 1) * DP], weight)
+            for (w, pair), weight in zip(jobs, weights)
+        ]
+        for (w, pair), got in zip(jobs, gots):
             for side in range(2):
                 mine = got[side * DP : (side + 1) * DP, side * TOK : (side + 1) * TOK]
                 mine = mine * (1.0 / mine[D : D + 1])
                 start = first_row + (2 * pair + side) * DP
-                o_s[w, start : start + DP] = mine.astype(BF16)
-
-    def project_own(w, carry):
-        x = xn[w]
-        q_s[w] = dot_nt(wq_s[...], x).astype(BF16)
-        k_s[w] = dot_nt(x, wk_s[...]).astype(BF16)
-        v_s[w] = dot_nt(wv_s[...], x).astype(BF16)
-        return carry
-
-    lax.fori_loop(0, windows, project_own, 0, unroll=4)
-
-    def self_window(w, carry):
-        attend(w, k_s[w], v_s[w], 0)
-        return carry
-
-    lax.fori_loop(0, windows, self_window, 0, unroll=2)
+                o_s[ws[w], start : start + DP] = mine.astype(BF16)
+
+    def project_own(g, carry):
+        ws = pl.ds(g * PROJ, PROJ)
+        x = xn[ws].reshape(PROJ * TOK, CP)
+        k_s[ws] = dot_nt(x, wk_s[...]).astype(BF16).reshape(PROJ, TOK, CP)
+        q = dot_nt(wq_s[...], x).astype(BF16)
+        v = dot_nt(wv_s[...], x).astype(BF16)
+        for i in range(PROJ):
+            q_s[g * PROJ + i] = q[:, i * TOK : (i + 1) * TOK]
+            v_s[g * PROJ + i] = v[:, i * TOK : (i + 1) * TOK]
+        return carry
+
+    lax.fori_loop(0, windows // PROJ, project_own, 0)
+
+    def self_window(g, carry):
+        ws = [g * GROUP + i for i in range(GROUP)]
+        attend(ws, [k_s[w] for w in ws], [v_s[w] for w in ws], 0)
+        return carry
+
+    lax.fori_loop(0, windows // GROUP, self_window, 0)
 
     wc_s[...] = jnp.zeros_like(wc_s)
     for layer in range(2):
@@ -197,26 +216,32 @@
     slot_next = jnp.where(has_next, 1, 0)
     own_rows = x_ref.shape[1] // (2 * WIN)
 
-    def project_both(w, carry):
-        x = jnp.concatenate([xin[slot_prev, w], xin[slot_next, w]], axis=0)
-        k2_s[w] = dot_nt(x, wk_s[...]).astype(BF16)
-        v2_s[w] = dot_nt(wv_s[...], x).astype(BF16)
-        return carry
-
-    def mutual_window(w, carry):
-        attend(w, k2_s[w], v2_s[w], HEADS * DP)
-        return carry
-
-    def finish_pair(p, carry):
-        both = []
-        for side in range(2):
-            w = 2 * p + side
-            mixed = dot(wp_s[...], o_s[w]).T
-            both.append(x_ref[w].astype(F32) + mixed[:, :C])
-        shaped = jnp.stack(both, axis=0).reshape(2, 2, own_rows, WIN, C)
-        shaped = shaped.transpose(1, 2, 0, 3, 4).reshape(2, own_rows, 2 * WIN, C)
-        cols = pl.ds(pl.multiple_of(p * 2 * WIN, 2 * WIN), 2 * WIN)
-        att[:, HALO : HALO + own_rows, cols, :C] = shaped.astype(BF16)
+    def project_both(g, carry):
+        ws = pl.ds(g * PROJ, PROJ)
+        for side, slot in ((0, slot_prev), (1, slot_next)):
+            x = xin[slot, ws].reshape(PROJ * TOK, CP)
+            part = pl.ds(side * TOK, TOK)
+            k2_s[ws, part] = dot_nt(x, wk_s[...]).astype(BF16).reshape(PROJ, TOK, CP)
+            v = dot_nt(wv_s[...], x).astype(BF16)
+            for i in range(PROJ):
+                v2_s[g * PROJ + i, :, part] = v[:, i * TOK : (i + 1) * TOK]
+        return carry
+
+    def mutual_window(g, carry):
+        ws = [g * GROUP + i for i in range(GROUP)]
+        attend(ws, [k2_s[w] for w in ws], [v2_s[w] for w in ws], HEADS * DP)
+        return carry
+
+    def finish_pair(g, carry):
+        ws = [g * FIN + i for i in range(FIN)]
+        mixed = [dot(wp_s[...], o_s[w]) for w in ws]
+        mixed = [m.T[:, :C] for m in mixed]
+        for i in range(0, FIN, 2):
+            both = [x_ref[ws[i + j]].astype(F32) + mixed[i + j] for j in range(2)]
+            shaped = jnp.stack(both, axis=0).reshape(2, 2, own_rows, WIN, C)
+            shaped = shaped.transpose(1, 2, 0, 3, 4).reshape(2, own_rows, 2 * WIN, C)
+            cols = pl.ds(pl.multiple_of((g * FIN + i) * WIN, 2 * WIN), 2 * WIN)
+            att[:, HALO : HALO + own_rows, cols, :C] = shaped.astype(BF16)
         return carry
 
     def halo_copy(side, k):
@@ -242,9 +267,9 @@
         def _(k=k):
             clip_copy(1, k).wait_recv()
 
-        lax.fori_loop(k * per, (k + 1) * per, project_both, 0, unroll=4)
-        lax.fori_loop(k * per, (k + 1) * per, mutual_window, 0, unroll=2)
-        lax.fori_loop(k * per // 2, (k + 1) * per // 2, finish_pair, 0, unroll=2)
+        lax.fori_loop(k * per // PROJ, (k + 1) * per // PROJ, project_both, 0)
+        lax.fori_loop(k * per // GROUP, (k + 1) * per // GROUP, mutual_window, 0)
+        lax.fori_loop(k * per // FIN, (k + 1) * per // FIN, finish_pair, 0)
 
         @pl.when(has_up)
         def _(k=k):
@@ -254,25 +279,43 @@
         def _(k=k):
             halo_copy(1, k).start()
 
-    def convolve(field, row, layer, f):
-        stacked = jnp.concatenate([field[f, row], field[f, row + 1], field[f, row + 2]], axis=1)
+    def convolve(field, jobs, layer):
+        stacked = jnp.concatenate(
+            [
+                jnp.concatenate([field[f, row + r] for r in range(3)], axis=1)
+                for f, row in jobs
+            ],
+            axis=0,
+        )
         part = dot_nt(stacked, wc_s[layer])
-        left_s[f, 8 : 8 + width] = part[:, :CP]
-        right_s[f, 0:width] = part[:, 2 * CP :]
-        return part[:, CP : 2 * CP] + left_s[f, 7 : 7 + width] + right_s[f, 1 : 1 + width]
-
-    def first_conv(row, carry):
-        for f in range(2):
-            inner[f, row] = jnp.maximum(convolve(att, row, 0, f), 0.0).astype(BF16)
-        return carry
-
-    def second_conv(row, carry):
-        for f in range(2):
-            total = att[f, row + HALO].astype(F32) + convolve(inner, row, 1, f)
+        for i in range(len(jobs)):
+            mine = part[i * width : (i + 1) * width]
+            left_s[i, 8 : 8 + width] = mine[:, :CP]
+            right_s[i, 0:width] = mine[:, 2 * CP :]
+        return [
+            part[i * width : (i + 1) * width, CP : 2 * CP]
+            + left_s[i, 7 : 7 + width]
+            + right_s[i, 1 : 1 + width]
+            for i in range(len(jobs))
+        ]
+
+    def conv_jobs(group):
+        return [(f, group * ROWS + i) for i in range(ROWS) for f in range(2)]
+
+    def first_conv(group, carry):
+        jobs = conv_jobs(group)
+        for (f, row), total in zip(jobs, convolve(att, jobs, 0)):
+            inner[f, row] = jnp.maximum(total, 0.0).astype(BF16)
+        return carry
+
+    def second_conv(group, carry):
+        jobs = conv_jobs(group)
+        for (f, row), total in zip(jobs, convolve(inner, jobs, 1)):
+            total = att[f, row + HALO].astype(F32) + total
             out_ref[f, row] = total[:, :C].astype(BF16)
         return carry
 
-    lax.fori_loop(HALO, own_rows, first_conv, 0)
+    lax.fori_loop(HALO // ROWS, own_rows // ROWS, first_conv, 0)
     for k in range(CHUNKS):
 
         @pl.when(has_down)
@@ -283,8 +326,8 @@
         def _(k=k):
             halo_copy(1, k).wait_recv()
 
-    lax.fori_loop(0, HALO, first_conv, 0)
-    lax.fori_loop(own_rows, own_rows + HALO, first_conv, 0)
+    lax.fori_loop(0, HALO // ROWS, first_conv, 0)
+    lax.fori_loop(own_rows // ROWS, (own_rows + HALO) // ROWS, first_conv, 0)
 
     @pl.when(jnp.logical_not(has_up))
     def _():
@@ -294,7 +337,7 @@
     def _():
         inner[:, own_rows + 1] = jnp.zeros_like(inner[:, 0])
 
-    lax.fori_loop(0, own_rows, second_conv, 0)
+    lax.fori_loop(0, own_rows // ROWS, second_conv, 0)
 
     for k in range(CHUNKS):
         for copy, low, high in ((clip_copy, has_next, has_prev), (halo_copy, has_up, has_down)):
@@ -337,8 +380,8 @@
             pltpu.VMEM((CP, 2 * HEADS * DP), BF16),
             pltpu.VMEM((2, 3 * CP, 3 * CP), BF16),
             pltpu.VMEM((HEADS, CP, TOK), BF16),
-            pltpu.VMEM((f, w + 16, CP), F32),
-            pltpu.VMEM((f, w + 16, CP), F32),
+            pltpu.VMEM((2 * ROWS, w + 16, CP), F32),
+            pltpu.VMEM((2 * ROWS, w + 16, CP), F32),
             pltpu.SemaphoreType.DMA((2, CHUNKS)),
             pltpu.SemaphoreType.DMA((2, CHUNKS)),
             pltpu.SemaphoreType.DMA((2, CHUNKS)),

time: 78.9 us -> 46.5 us (0.59)
  Pallas kernels: 73.9 us -> 41.4 us
    pallas_call x1, Pallas kernels: 73.9 us -> 41.4 us  [shards(): pl.pallas_call(functools.partial(kernel, clips, parts), out_shape=jax.Sha...]
where the time goes in v2:
time: 46.5 us; the launch traced here: 46 us
  Pallas kernels  41.4 us (89%)
  local copies, waits for them, and re-layouts  4.55 us (10%)
    pallas_call x1, Pallas kernels, shards(): pl.pallas_call(functools.partial(kernel, clips, parts), out_shape=jax.Sha...  41.4 us
    unnamed x9, local copies, waits for them, and re-layouts  2.63 us
    transpose x1, local copies, waits for them, and re-layouts, shards(): return restored.transpose(3, 0, 1, 2)  1.64 us

profile of v2, /device:TPU:17, one launch (start us, length us, event | category | flops | bytes accessed | tf_op | source)
XLA Modules:
  0.0 46.0 jit_solution(6405524614156373869)
XLA Ops:
  0.0 1.9 %copy.8 = bf16[120,2,8,256]{0,3,2,1:T(8,128)(2,1)S(1)} copy(bf16[120,2,8,256]{3,2,1,0:T(8,128)(2,1)} %param.5) | data formatting | bytes 1966080 | tf_op args[0]
  1.9 0.0 copy-start
  1.9 0.0 copy-start.1
  1.9 0.0 copy-start.2
  1.9 0.3 copy.9
  2.2 0.0 copy-start.3
  2.2 0.7 %copy-done = bf16[2,3,3,120,120]{4,3,2,1,0:T(8,128)(2,1)S(1)} copy-done((bf16[2,3,3,120,120]{4,3,2,1,0:T(8,128)(2,1)S(1)}, bf16[2,3,3,120,120]{4,3,2,1,0:T(8,128)(2,1)}, u32[]{:S(2)}) %copy-start) | copy-done | bytes 518424
  3.0 0.0 copy-done.1
  3.0 0.0 copy-done.2
  3.0 0.0 copy-done.3
  3.0 41.4 %shard_map.55 = bf16[2,8,256,120]{3,2,1,0:T(8,128)(2,1)S(1)} custom-call(bf16[32,128,120]{2,1,0:T(8,128)(2,1)S(1)} %bitcast.6, f32[1,120]{1,0:T(1,128)S(1)} %bitcast.8, bf16[360,120]{1,0:T(8,128)(2,1)S(1)} %copy-done.1, bf16[120,240]{1,0:T(8,128)(2,1)S(1)} %copy-done.2, bf16[2,3,3,120,120]{4,3,2,1,0:T(8,128)(2,1)S(1)} %copy-done), custom_call_target="tpu_custom_call" | custom-call | tf_op jit(solution)/shard_map/pallas_call | solution.py:361
  44.4 1.6 %copy.10 = bf16[120,2,8,256]{3,2,1,0:T(8,128)(2,1)} copy(bf16[120,2,8,256]{0,3,2,1:T(8,128)(2,1)S(1)} %bitcast.7) | data formatting | bytes 1966080 | tf_op jit(solution)/shard_map/transpose | solution.py:394
Async XLA Ops:
  1.9 1.1 %copy-start = (bf16[2,3,3,120,120]{4,3,2,1,0:T(8,128)(2,1)S(1)}, bf16[2,3,3,120,120]{4,3,2,1,0:T(8,128)(2,1)}, u32[]{:S(2)}) copy-start(bf16[2,3,3,120,120]{4,3,2,1,0:T(8,128)(2,1)} %wconv_ref.1) | copy-start | bytes 1555204
  1.9 1.0 %copy-start.1 = (bf16[360,120]{1,0:T(8,128)(2,1)S(1)}, bf16[360,120]{1,0:T(8,128)(2,1)}, u32[]{:S(2)}) copy-start(bf16[360,120]{1,0:T(8,128)(2,1)} %wqkv_ref.1) | copy-start | bytes 259204
  1.9 1.0 %copy-start.2 = (bf16[120,240]{1,0:T(8,128)(2,1)S(1)}, bf16[120,240]{1,0:T(8,128)(2,1)}, u32[]{:S(2)}) copy-start(bf16[120,240]{1,0:T(8,128)(2,1)} %wproj_ref.1) | copy-start | bytes 172804
  2.2 0.7 %copy-start.3 = (f32[120]{0:T(128)S(1)}, f32[120]{0:T(128)}, u32[]{:S(2)}) copy-start(f32[120]{0:T(128)} %param.6) | copy-start | bytes 1444

commit v3 on v1

v3 whole, which is shorter than its diff:
```python
import functools
import math

import jax
import jax.numpy as jnp
from jax import lax
from jax.experimental import pallas as pl
from jax.experimental.pallas import tpu as pltpu
from jax.sharding import PartitionSpec as P

HEADS = 6
WIN = 8
C = 120
D = C // HEADS
CP = 128
DP = 32
TOK = 2 * WIN * WIN
HALO = 2
CUTS = (8, 8, 8, 4, 4)
GROUP = 8
LAG = 16
LAG1 = 4
LAG2 = 6
LAG3 = 8
MESH = pl.DeviceIdType.MESH
F32 = jnp.float32
BF16 = jnp.bfloat16


def dot(a, b):
    return lax.dot_general(a, b, (((1,), (0,)), ((), ())), preferred_element_type=F32)


def dot_nt(a, b):
    return lax.dot_general(a, b, (((1,), (1,)), ((), ())), preferred_element_type=F32)


def iota(shape, dim):
    return lax.broadcasted_iota(jnp.int32, shape, dim)


def one_hot_heads(rows, cols, padded_dim):
    padded = iota((rows, cols), padded_dim)
    packed = iota((rows, cols), 1 - padded_dim)
    entry = padded & (DP - 1)
    hit = ((padded >> 5) * D + entry == packed) & (entry < D)
    return jnp.where(hit, 1.0, 0.0).astype(BF16)


def pad_rows(value, rows):
    extra = jnp.zeros((rows - value.shape[0], value.shape[1]), value.dtype)
    return jnp.concatenate([value, extra], axis=0)


def kernel(
    clips,
    parts,
    x_ref,
    gain_ref,
    wqkv_ref,
    wproj_ref,
    wconv_ref,
    out_ref,
    xn,
    xin,
    q_s,
    k_s,
    v_s,
    k2_s,
    v2_s,
    o_s,
    att,
    inner,
    wq_s,
    wk_s,
    wv_s,
    wp_s,
    wc_s,
    mask_s,
    left1_s,
    middle1_s,
    right1_s,
    left2_s,
    middle2_s,
    right2_s,
    wconv_s,
    weights_sem,
    send_sem,
    recv_sem,
    hsend_sem,
    hrecv_sem,
):
    me = lax.axis_index("clip")
    ha = lax.axis_index("ha")
    width = x_ref.shape[2]
    windows = width // WIN
    own_rows = x_ref.shape[1]
    spans = []
    for size in CUTS:
        start = sum(CUTS[: len(spans)])
        spans.append((start, start + size))
    has_prev, has_next = me > 0, me < clips - 1
    has_up, has_down = ha > 0, ha < parts - 1

    weights_copy = pltpu.make_async_copy(wconv_ref, wconv_s, weights_sem)
    weights_copy.start()
    att[...] = jnp.zeros_like(att)
    lane_one = jnp.where(iota((TOK, CP), 1) == C, 1.0, 0.0).astype(BF16)

    barrier = pltpu.get_barrier_semaphore()
    neighbours = (
        (has_prev, (me - 1, ha)),
        (has_next, (me + 1, ha)),
        (has_up, (me, ha - 1)),
        (has_down, (me, ha + 1)),
    )
    for there, device in neighbours:

        @pl.when(there)
        def _(device=device):
            pl.semaphore_signal(barrier, inc=1, device_id=device, device_id_type=MESH)

    wqkv = wqkv_ref[...].astype(F32)
    for slot, start in ((wq_s, 0), (wk_s, C)):
        slot[...] = jnp.zeros_like(slot)
        slot[:, :C] = pad_rows(wqkv[start : start + C], CP).astype(BF16)
    wv = dot(one_hot_heads(HEADS * DP, C, 0), wqkv[2 * C :].astype(BF16))
    ones_row = (iota((HEADS * DP, CP), 0) & (DP - 1) == D) & (iota((HEADS * DP, CP), 1) == C)
    wv_s[...] = jnp.where(ones_row, 1.0, 0.0).astype(BF16)
    wv_s[:, :C] = wv.astype(BF16)
    wp = dot(wproj_ref[...], one_hot_heads(2 * C, 2 * HEADS * DP, 1))
    wp_s[...] = pad_rows(wp, CP).astype(BF16)
    channel = iota((CP, TOK), 0)
    for h in range(HEADS):
        mask_s[h] = jnp.where((channel >= h * D) & (channel < (h + 1) * D), 1.0, 0.0).astype(BF16)

    gain = gain_ref[...]

    def norm_pair(p, carry):
        cols = pl.ds(pl.multiple_of(p * 2 * WIN, 2 * WIN), 2 * WIN)
        x = x_ref[:, :, cols].astype(F32).reshape(2, own_rows, 2, WIN, C)
        x = x.transpose(2, 0, 1, 3, 4).reshape(2, TOK, C)
        centred = x - jnp.mean(x, axis=-1, keepdims=True)
        spread = jnp.mean(centred * centred, axis=-1, keepdims=True)
        normed = centred * lax.rsqrt(spread + 1e-05) * gain
        for i in range(2):
            xn[2 * p + i] = lane_one
        xn[pl.ds(2 * p, 2), :, :C] = normed.astype(BF16)
        return carry

    def clip_copy(side, k):
        first, last = spans[k]
        part = pl.ds(first, last - first)
        return pltpu.make_async_remote_copy(
            src_ref=xn.at[part],
            dst_ref=xin.at[side, part],
            send_sem=send_sem.at[side, k],
            recv_sem=recv_sem.at[side, k],
            device_id=(me + 1 - 2 * side, ha),
            device_id_type=MESH,
        )

    for k, (first, last) in enumerate(spans):
        lax.fori_loop(first // 2, last // 2, norm_pair, 0, unroll=2)
        if k == 0:
            pl.semaphore_wait(barrier, sum(jnp.where(there, 1, 0) for there, _ in neighbours))

        @pl.when(has_next)
        def _(k=k):
            clip_copy(0, k).start()

        @pl.when(has_prev)
        def _(k=k):
            clip_copy(1, k).start()

    scale = math.log2(math.e) / math.sqrt(D)

    def attend(ws, keys, values, first_row):
        jobs = [(w, pair) for w in range(len(ws)) for pair in range(HEADS // 2)]
        qs = [q_s[w] for w in ws]
        scores, weights, gots = {}, {}, {}

        def score(j):
            w, pair = jobs[j]
            queries = jnp.concatenate(
                [qs[w] * mask_s[2 * pair], qs[w] * mask_s[2 * pair + 1]], axis=1
            )
            scores[j] = dot(keys[w], queries)

        def weigh(j):
            got = scores.pop(j)
            peak = jnp.max(got, axis=0, keepdims=True)
            weights[j] = jnp.exp2((got - peak) * scale).astype(BF16)

        def gather(j):
            w, pair = jobs[j]
            gots[j] = dot(values[w][2 * pair * DP : 2 * (pair + 1) * DP], weights.pop(j))

        def store(j):
            w, pair = jobs[j]
            got = gots.pop(j)
            for side in range(2):
                mine = got[side * DP : (side + 1) * DP, side * TOK : (side + 1) * TOK]
                mine = mine * (1.0 / mine[D : D + 1])
                start = first_row + (2 * pair + side) * DP
                o_s[ws[w], start : start + DP] = mine.astype(BF16)

        n = len(jobs)
        for t in range(n + LAG2 + LAG3):
            if t < n:
                score(t)
            if 0 <= t - LAG1 < n:
                weigh(t - LAG1)
            if 0 <= t - LAG2 < n:
                gather(t - LAG2)
            if 0 <= t - LAG3 < n:
                store(t - LAG3)

    def project_own(g, carry):
        ws = pl.ds(g * GROUP, GROUP)
        x = xn[ws].reshape(GROUP * TOK, CP)
        k_s[ws] = dot_nt(x, wk_s[...]).astype(BF16).reshape(GROUP, TOK, CP)
        q = dot_nt(wq_s[...], x).astype(BF16)
        v = dot_nt(wv_s[...], x).astype(BF16)
        for i in range(GROUP):
            q_s[g * GROUP + i] = q[:, i * TOK : (i + 1) * TOK]
            v_s[g * GROUP + i] = v[:, i * TOK : (i + 1) * TOK]
        return carry

    lax.fori_loop(0, windows // GROUP, project_own, 0)

    def self_window(g, carry):
        ws = [g * GROUP + i for i in range(GROUP)]
        attend(ws, [k_s[w] for w in ws], [v_s[w] for w in ws], 0)
        return carry

    lax.fori_loop(0, windows // GROUP, self_window, 0)

    weights_copy.wait()
    wc_s[...] = jnp.zeros_like(wc_s)
    for layer in range(2):
        for r in range(3):
            for s in range(3):
                weight = pad_rows(wconv_s[layer, r, s].astype(F32), CP).astype(BF16)
                wc_s[layer, s * CP : (s + 1) * CP, r * CP : r * CP + C] = weight
    for slot, row in ((left1_s, 0), (left2_s, 0), (right1_s, width), (right2_s, width)):
        slot[:, row : row + 8] = jnp.zeros((slot.shape[0], 8, CP), F32)

    slot_prev = jnp.where(has_prev, 0, 1)
    slot_next = jnp.where(has_next, 1, 0)

    def mutual_chunk(first, last):
        ws = pl.ds(first, last - first)
        for side, slot in ((0, slot_prev), (1, slot_next)):
            x = xin[slot, ws].reshape((last - first) * TOK, CP)
            part = slice(side * TOK, (side + 1) * TOK)
            k2_s[ws, part] = dot_nt(x, wk_s[...]).astype(BF16).reshape(last - first, TOK, CP)
            v = dot_nt(wv_s[...], x).astype(BF16)
            for i in range(last - first):
                v2_s[first + i, :, part] = v[:, i * TOK : (i + 1) * TOK]
        every = list(range(first, last))
        attend(every, [k2_s[w] for w in every], [v2_s[w] for w in every], HEADS * DP)
        mixed = [dot(wp_s[...], o_s[w]) for w in every]
        mixed = [m.T[:, :C] for m in mixed]
        for i in range(0, len(every), 2):
            shaped = jnp.stack(mixed[i : i + 2], axis=0).reshape(2, 2, own_rows, WIN, C)
            shaped = shaped.transpose(1, 2, 0, 3, 4).reshape(2, own_rows, 2 * WIN, C)
            cols = slice(every[i] * WIN, every[i] * WIN + 2 * WIN)
            total = x_ref[:, :, cols].astype(F32) + shaped
            att[:, HALO : HALO + own_rows, cols, :C] = total.astype(BF16)

    def halo_copy(side, k):
        first, last = spans[k]
        cols = pl.ds(first * WIN, (last - first) * WIN)
        src_row = own_rows if side else HALO
        dst_row = 0 if side else HALO + own_rows
        return pltpu.make_async_remote_copy(
            src_ref=att.at[:, pl.ds(src_row, HALO), cols],
            dst_ref=att.at[:, pl.ds(dst_row, HALO), cols],
            send_sem=hsend_sem.at[side, k],
            recv_sem=hrecv_sem.at[side, k],
            device_id=(me, ha + (1 if side else -1)),
            device_id_type=MESH,
        )

    def products(field, jobs, layer, slots, start, stop):
        stacked = jnp.concatenate(
            [
                jnp.concatenate([field[f, row + r, start:stop] for r in range(3)], axis=1)
                for f, row in jobs
            ],
            axis=0,
        )
        part = dot_nt(stacked, wc_s[layer])
        size = stop - start
        left, middle, right = slots
        for i, (f, row) in enumerate(jobs):
            job = f * (own_rows + 2) + row
            mine = part[i * size : (i + 1) * size]
            left[job, 8 + start : 8 + stop] = mine[:, :CP]
            middle[job, start:stop] = mine[:, CP : 2 * CP]
            right[job, start:stop] = mine[:, 2 * CP :]

    def summed(slots, f, row, start, stop):
        left, middle, right = slots
        job = f * (own_rows + 2) + row
        return (
            middle[job, start:stop]
            + left[job, 7 + start : 7 + stop]
            + right[job, 1 + start : 1 + stop]
        )

    slots1, slots2 = (left1_s, middle1_s, right1_s), (left2_s, middle2_s, right2_s)

    def behind(start, stop):
        return max(0, start - LAG), (stop if stop == width else stop - LAG)

    def grid(rows):
        return [(f, row) for row in rows for f in range(2)]

    def wait_halo(k):
        @pl.when(has_down)
        def _():
            halo_copy(0, k).wait_recv()

        @pl.when(has_up)
        def _():
            halo_copy(1, k).wait_recv()

    def conv_rows(rows1, rows2, start, stop):
        products(att, grid(rows1), 0, slots1, start, stop)
        start, stop = behind(start, stop)
        for f, row in grid(rows1):
            total = jnp.maximum(summed(slots1, f, row, start, stop), 0.0)
            if row == 0:
                total = jnp.where(has_up, total, 0.0)
            if row == own_rows + 1:
                total = jnp.where(has_down, total, 0.0)
            inner[f, row, start:stop] = total.astype(BF16)
        products(inner, grid(rows2), 1, slots2, start, stop)
        start, stop = behind(start, stop)
        for f, row in grid(rows2):
            total = att[f, row + HALO, start:stop].astype(F32)
            total = total + summed(slots2, f, row, start, stop)
            out_ref[f, row, start:stop] = total[:, :C].astype(BF16)

    def conv_inside(k):
        rows1, rows2 = range(2, own_rows), range(2, own_rows - 2)
        conv_rows(rows1, rows2, spans[k][0] * WIN, spans[k][1] * WIN)

    for k, (first, last) in enumerate(spans):
        if k > 0:
            conv_inside(k - 1)

        @pl.when(has_prev)
        def _(k=k):
            clip_copy(0, k).wait_recv()

        @pl.when(has_next)
        def _(k=k):
            clip_copy(1, k).wait_recv()

        mutual_chunk(first, last)

        @pl.when(has_up)
        def _(k=k):
            halo_copy(0, k).start()

        @pl.when(has_down)
        def _(k=k):
            halo_copy(1, k).start()

    conv_inside(len(spans) - 1)
    for k in range(len(spans)):
        wait_halo(k)
    last_row = own_rows - 1
    conv_rows(
        (0, 1, own_rows, own_rows + 1), (0, 1, last_row - 1, last_row), 0, width
    )

    for k in range(len(spans)):
        for copy, low, high in ((clip_copy, has_next, has_prev), (halo_copy, has_up, has_down)):

            @pl.when(low)
            def _(copy=copy, k=k):
                copy(0, k).wait_send()

            @pl.when(high)
            def _(copy=copy, k=k):
                copy(1, k).wait_send()


def shards(frames, ln_gain, w_qkv, w_proj, conv_weight):
    c, f, h, w = frames.shape
    windows = w // WIN
    clips, parts = lax.axis_size("clip"), lax.axis_size("ha")
    tokens = frames.transpose(1, 2, 3, 0)
    vmem = pl.BlockSpec(memory_space=pltpu.VMEM)
    restored = pl.pallas_call(
        functools.partial(kernel, clips, parts),
        out_shape=jax.ShapeDtypeStruct((f, h, w, c), BF16),
        in_specs=[vmem] * 4 + [pl.BlockSpec(memory_space=pl.ANY)],
        out_specs=vmem,
        scratch_shapes=[
            pltpu.VMEM((windows, TOK, CP), BF16),
            pltpu.VMEM((2, windows, TOK, CP), BF16),
            pltpu.VMEM((windows, CP, TOK), BF16),
            pltpu.VMEM((windows, TOK, CP), BF16),
            pltpu.VMEM((windows, HEADS * DP, TOK), BF16),
            pltpu.VMEM((windows, 2 * TOK, CP), BF16),
            pltpu.VMEM((windows, HEADS * DP, 2 * TOK), BF16),
            pltpu.VMEM((windows, 2 * HEADS * DP, TOK), BF16),
            pltpu.VMEM((f, h + 2 * HALO, w, CP), BF16),
            pltpu.VMEM((f, h + 2, w, CP), BF16),
            pltpu.VMEM((CP, CP), BF16),
            pltpu.VMEM((CP, CP), BF16),
            pltpu.VMEM((HEADS * DP, CP), BF16),
            pltpu.VMEM((CP, 2 * HEADS * DP), BF16),
            pltpu.VMEM((2, 3 * CP, 3 * CP), BF16),
            pltpu.VMEM((HEADS, CP, TOK), BF16),
            *[pltpu.VMEM((f * (h + 2), w + 16, CP), F32) for _ in range(6)],
            pltpu.VMEM(conv_weight.shape, BF16),
            pltpu.SemaphoreType.DMA,
            pltpu.SemaphoreType.DMA((2, len(CUTS))),
            pltpu.SemaphoreType.DMA((2, len(CUTS))),
            pltpu.SemaphoreType.DMA((2, len(CUTS))),
            pltpu.SemaphoreType.DMA((2, len(CUTS))),
        ],
        compiler_params=pltpu.CompilerParams(
            collective_id=0, has_side_effects=True, vmem_limit_bytes=48 * 1024 * 1024
        ),
    )(tokens, ln_gain.reshape(1, c), w_qkv, w_proj, conv_weight)
    return restored.transpose(3, 0, 1, 2)


def solution(mesh):
    return jax.shard_map(
        shards,
        mesh=mesh,
        in_specs=(P(None, "clip", "ha", None), P(), P(), P(), P()),
        out_specs=P(None, "clip", "ha", None),
        check_vma=False,
    )
```

time: 78.9 us -> 43.2 us (0.55)
  Pallas kernels: 73.9 us -> 38.8 us
    pallas_call x1, Pallas kernels: 73.9 us -> 38.8 us  [shards(): pl.pallas_call(functools.partial(kernel, clips, parts), out_shape=jax.Sha...]
where the time goes in v3:
time: 43.2 us; the launch traced here: 43.1 us
  Pallas kernels  38.8 us (90%)
  local copies, waits for them, and re-layouts  4.23 us (10%)
    pallas_call x1, Pallas kernels, shards(): pl.pallas_call(functools.partial(kernel, clips, parts), out_shape=jax.Sha...  38.8 us
    unnamed x9, local copies, waits for them, and re-layouts  2.59 us
    transpose x1, local copies, waits for them, and re-layouts, shards(): return restored.transpose(3, 0, 1, 2)  1.64 us

profile of v3, /device:TPU:17, one launch (start us, length us, event | category | flops | bytes accessed | tf_op | source)
XLA Modules:
  0.0 43.1 jit_solution(1549715279988622579)
XLA Ops:
  0.0 0.0 copy-start
  0.0 0.0 copy-start.1
  0.0 0.0 copy-start.2
  0.0 2.0 %copy.6 = bf16[120,2,8,256]{0,3,2,1:T(8,128)(2,1)S(1)} copy(bf16[120,2,8,256]{3,2,1,0:T(8,128)(2,1)} %param.5) | data formatting | bytes 1966080 | tf_op args[0]
  2.0 0.0 copy-start.3
  2.0 0.0 copy-done
  2.0 0.0 copy-done.1
  2.0 0.0 copy-done.2
  2.0 0.6 %copy-done.3 = f32[120]{0:T(128)S(1)} copy-done((f32[120]{0:T(128)S(1)}, f32[120]{0:T(128)}, u32[]{:S(2)}) %copy-start.3) | copy-done | bytes 504
  2.6 38.8 %shard_map.55 = bf16[2,8,256,120]{3,2,1,0:T(8,128)(2,1)S(1)} custom-call(bf16[2,8,256,120]{3,2,1,0:T(8,128)(2,1)S(1)} %bitcast.4, f32[1,120]{1,0:T(1,128)S(1)} %bitcast.5, bf16[360,120]{1,0:T(8,128)(2,1)S(1)} %copy-done.1, bf16[120,240]{1,0:T(8,128)(2,1)S(1)} %copy-done.2, bf16[2,3,3,120,120]{4,3,2,1,0:T(8,128)(2,1)S(1)} %copy-done), custom_call_target="tpu_custom_call" | custom-call | tf_op jit(solution)/shard_map/pallas_call | solution.py:399
  41.4 1.6 %copy.7 = bf16[120,2,8,256]{3,2,1,0:T(8,128)(2,1)} copy(bf16[120,2,8,256]{0,3,2,1:T(8,128)(2,1)S(1)} %bitcast.3) | data formatting | bytes 1966080 | tf_op jit(solution)/shard_map/transpose | solution.py:433
Async XLA Ops:
  0.0 2.0 %copy-start = (bf16[2,3,3,120,120]{4,3,2,1,0:T(8,128)(2,1)S(1)}, bf16[2,3,3,120,120]{4,3,2,1,0:T(8,128)(2,1)}, u32[]{:S(2)}) copy-start(bf16[2,3,3,120,120]{4,3,2,1,0:T(8,128)(2,1)} %wconv_ref.1) | copy-start | bytes 1555204
  0.0 2.0 %copy-start.1 = (bf16[360,120]{1,0:T(8,128)(2,1)S(1)}, bf16[360,120]{1,0:T(8,128)(2,1)}, u32[]{:S(2)}) copy-start(bf16[360,120]{1,0:T(8,128)(2,1)} %wqkv_ref.1) | copy-start | bytes 259204
  0.0 2.0 %copy-start.2 = (bf16[120,240]{1,0:T(8,128)(2,1)S(1)}, bf16[120,240]{1,0:T(8,128)(2,1)}, u32[]{:S(2)}) copy-start(bf16[120,240]{1,0:T(8,128)(2,1)} %wproj_ref.1) | copy-start | bytes 172804
  2.0 0.7 %copy-start.3 = (f32[120]{0:T(128)S(1)}, f32[120]{0:T(128)}, u32[]{:S(2)}) copy-start(f32[120]{0:T(128)} %param.6) | copy-start | bytes 1444

commit v4 on v3

--- a/solution.py
+++ b/solution.py
@@ -62,6 +62,7 @@
     wconv_ref,
     out_ref,
     xn,
+    sent,
     xin,
     q_s,
     k_s,
@@ -83,8 +84,6 @@
     left2_s,
     middle2_s,
     right2_s,
-    wconv_s,
-    weights_sem,
     send_sem,
     recv_sem,
     hsend_sem,
@@ -102,9 +101,6 @@
     has_prev, has_next = me > 0, me < clips - 1
     has_up, has_down = ha > 0, ha < parts - 1
 
-    weights_copy = pltpu.make_async_copy(wconv_ref, wconv_s, weights_sem)
-    weights_copy.start()
-    att[...] = jnp.zeros_like(att)
     lane_one = jnp.where(iota((TOK, CP), 1) == C, 1.0, 0.0).astype(BF16)
 
     barrier = pltpu.get_barrier_semaphore()
@@ -119,6 +115,58 @@
         @pl.when(there)
         def _(device=device):
             pl.semaphore_signal(barrier, inc=1, device_id=device, device_id_type=MESH)
+
+    gain = gain_ref[...].reshape(1, C)
+
+    def norm_pair(p, carry):
+        cols = pl.ds(pl.multiple_of(p * 2 * WIN, 2 * WIN), 2 * WIN)
+        x = x_ref[:, :, cols].astype(F32).reshape(2, own_rows, 2, WIN, C)
+        x = x.transpose(2, 0, 1, 3, 4).reshape(2, TOK, C)
+        centred = x - jnp.mean(x, axis=-1, keepdims=True)
+        spread = jnp.mean(centred * centred, axis=-1, keepdims=True)
+        normed = centred * lax.rsqrt(spread + 1e-05) * gain
+        for i in range(2):
+            xn[2 * p + i] = lane_one
+        xn[pl.ds(2 * p, 2), :, :C] = normed.astype(BF16)
+        packed = jnp.concatenate([normed[0].T, normed[1].T], axis=0)
+        sent[pl.ds(pl.multiple_of(p * 2 * C, 2 * C), 2 * C)] = packed.astype(BF16)
+        return carry
+
+    def clip_copy(side, k):
+        first, last = spans[k]
+        part = pl.ds(first * C, (last - first) * C)
+        return pltpu.make_async_remote_copy(
+            src_ref=sent.at[part],
+            dst_ref=xin.at[side, part],
+            send_sem=send_sem.at[side, k],
+            recv_sem=recv_sem.at[side, k],
+            device_id=(me + 1 - 2 * side, ha),
+            device_id_type=MESH,
+        )
+
+    for k, (first, last) in enumerate(spans):
+        lax.fori_loop(first // 2, last // 2, norm_pair, 0, unroll=2)
+        if k == 0:
+            pl.semaphore_wait(barrier, sum(jnp.where(there, 1, 0) for there, _ in neighbours))
+
+        @pl.when(has_next)
+        def _(k=k):
+            clip_copy(0, k).start()
+
+        @pl.when(has_prev)
+        def _(k=k):
+            clip_copy(1, k).start()
+
+    own = slice(HALO, HALO + own_rows)
+    att[:, own] = jnp.zeros((2, own_rows, width, CP), BF16)
+
+    @pl.when(jnp.logical_not(has_up))
+    def _():
+        att[:, :HALO] = jnp.zeros((2, HALO, width, CP), BF16)
+
+    @pl.when(jnp.logical_not(has_down))
+    def _():
+        att[:, HALO + own_rows :] = jnp.zeros((2, HALO, width, CP), BF16)
 
     wqkv = wqkv_ref[...].astype(F32)
     for slot, start in ((wq_s, 0), (wk_s, C)):
@@ -134,45 +182,6 @@
     for h in range(HEADS):
         mask_s[h] = jnp.where((channel >= h * D) & (channel < (h + 1) * D), 1.0, 0.0).astype(BF16)
 
-    gain = gain_ref[...]
-
-    def norm_pair(p, carry):
-        cols = pl.ds(pl.multiple_of(p * 2 * WIN, 2 * WIN), 2 * WIN)
-        x = x_ref[:, :, cols].astype(F32).reshape(2, own_rows, 2, WIN, C)
-        x = x.transpose(2, 0, 1, 3, 4).reshape(2, TOK, C)
-        centred = x - jnp.mean(x, axis=-1, keepdims=True)
-        spread = jnp.mean(centred * centred, axis=-1, keepdims=True)
-        normed = centred * lax.rsqrt(spread + 1e-05) * gain
-        for i in range(2):
-            xn[2 * p + i] = lane_one
-        xn[pl.ds(2 * p, 2), :, :C] = normed.astype(BF16)
-        return carry
-
-    def clip_copy(side, k):
-        first, last = spans[k]
-        part = pl.ds(first, last - first)
-        return pltpu.make_async_remote_copy(
-            src_ref=xn.at[part],
-            dst_ref=xin.at[side, part],
-            send_sem=send_sem.at[side, k],
-            recv_sem=recv_sem.at[side, k],
-            device_id=(me + 1 - 2 * side, ha),
-            device_id_type=MESH,
-        )
-
-    for k, (first, last) in enumerate(spans):
-        lax.fori_loop(first // 2, last // 2, norm_pair, 0, unroll=2)
-        if k == 0:
-            pl.semaphore_wait(barrier, sum(jnp.where(there, 1, 0) for there, _ in neighbours))
-
-        @pl.when(has_next)
-        def _(k=k):
-            clip_copy(0, k).start()
-
-        @pl.when(has_prev)
-        def _(k=k):
-            clip_copy(1, k).start()
-
     scale = math.log2(math.e) / math.sqrt(D)
 
     def attend(ws, keys, values, first_row):
@@ -236,12 +245,11 @@
 
     lax.fori_loop(0, windows // GROUP, self_window, 0)
 
-    weights_copy.wait()
     wc_s[...] = jnp.zeros_like(wc_s)
     for layer in range(2):
         for r in range(3):
             for s in range(3):
-                weight = pad_rows(wconv_s[layer, r, s].astype(F32), CP).astype(BF16)
+                weight = pad_rows(wconv_ref[layer, r, s].astype(F32), CP).astype(BF16)
                 wc_s[layer, s * CP : (s + 1) * CP, r * CP : r * CP + C] = weight
     for slot, row in ((left1_s, 0), (left2_s, 0), (right1_s, width), (right2_s, width)):
         slot[:, row : row + 8] = jnp.zeros((slot.shape[0], 8, CP), F32)
@@ -249,10 +257,17 @@
     slot_prev = jnp.where(has_prev, 0, 1)
     slot_next = jnp.where(has_next, 1, 0)
 
+    top = jnp.where(iota((CP - C, TOK), 0) == 0, 1.0, 0.0)
+
     def mutual_chunk(first, last):
         ws = pl.ds(first, last - first)
         for side, slot in ((0, slot_prev), (1, slot_next)):
-            x = xin[slot, ws].reshape((last - first) * TOK, CP)
+            x = []
+            for w in range(first, last, 2):
+                both = xin[slot, w * C : (w + 2) * C].astype(F32)
+                for i in range(2):
+                    x.append(jnp.concatenate([both[i * C : (i + 1) * C], top], axis=0).T)
+            x = jnp.concatenate(x, axis=0).astype(BF16)
             part = slice(side * TOK, (side + 1) * TOK)
             k2_s[ws, part] = dot_nt(x, wk_s[...]).astype(BF16).reshape(last - first, TOK, CP)
             v = dot_nt(wv_s[...], x).astype(BF16)
@@ -344,13 +359,14 @@
             total = total + summed(slots2, f, row, start, stop)
             out_ref[f, row, start:stop] = total[:, :C].astype(BF16)
 
-    def conv_inside(k):
-        rows1, rows2 = range(2, own_rows), range(2, own_rows - 2)
-        conv_rows(rows1, rows2, spans[k][0] * WIN, spans[k][1] * WIN)
-
+    def conv_inside(start, stop):
+        conv_rows(range(2, own_rows), range(2, own_rows - 2), start, stop)
+
+    done = 0
     for k, (first, last) in enumerate(spans):
-        if k > 0:
-            conv_inside(k - 1)
+        if k > 1:
+            conv_inside(done, first * WIN)
+            done = first * WIN
 
         @pl.when(has_prev)
         def _(k=k):
@@ -370,13 +386,14 @@
         def _(k=k):
             halo_copy(1, k).start()
 
-    conv_inside(len(spans) - 1)
-    for k in range(len(spans)):
+    conv_inside(done, width)
+    rows1 = (0, 1, own_rows, own_rows + 1)
+    rows2 = (0, 1, own_rows - 2, own_rows - 1)
+    for k in range(len(spans) - 1):
         wait_halo(k)
-    last_row = own_rows - 1
-    conv_rows(
-        (0, 1, own_rows, own_rows + 1), (0, 1, last_row - 1, last_row), 0, width
-    )
+    conv_rows(rows1, rows2, 0, spans[-1][0] * WIN)
+    wait_halo(len(spans) - 1)
+    conv_rows(rows1, rows2, spans[-1][0] * WIN, width)
 
     for k in range(len(spans)):
         for copy, low, high in ((clip_copy, has_next, has_prev), (halo_copy, has_up, has_down)):
@@ -399,11 +416,12 @@
     restored = pl.pallas_call(
         functools.partial(kernel, clips, parts),
         out_shape=jax.ShapeDtypeStruct((f, h, w, c), BF16),
-        in_specs=[vmem] * 4 + [pl.BlockSpec(memory_space=pl.ANY)],
+        in_specs=[vmem] * 5,
         out_specs=vmem,
         scratch_shapes=[
             pltpu.VMEM((windows, TOK, CP), BF16),
-            pltpu.VMEM((2, windows, TOK, CP), BF16),
+            pltpu.VMEM((windows * c, TOK), BF16),
+            pltpu.VMEM((2, windows * c, TOK), BF16),
             pltpu.VMEM((windows, CP, TOK), BF16),
             pltpu.VMEM((windows, TOK, CP), BF16),
             pltpu.VMEM((windows, HEADS * DP, TOK), BF16),
@@ -419,8 +437,6 @@
             pltpu.VMEM((2, 3 * CP, 3 * CP), BF16),
             pltpu.VMEM((HEADS, CP, TOK), BF16),
             *[pltpu.VMEM((f * (h + 2), w + 16, CP), F32) for _ in range(6)],
-            pltpu.VMEM(conv_weight.shape, BF16),
-            pltpu.SemaphoreType.DMA,
             pltpu.SemaphoreType.DMA((2, len(CUTS))),
             pltpu.SemaphoreType.DMA((2, len(CUTS))),
             pltpu.SemaphoreType.DMA((2, len(CUTS))),
@@ -429,7 +445,7 @@
         compiler_params=pltpu.CompilerParams(
             collective_id=0, has_side_effects=True, vmem_limit_bytes=48 * 1024 * 1024
         ),
-    )(tokens, ln_gain.reshape(1, c), w_qkv, w_proj, conv_weight)
+    )(tokens, ln_gain, w_qkv, w_proj, conv_weight)
     return restored.transpose(3, 0, 1, 2)
 
 

time: 43.2 us -> 40.9 us (0.947); the launches traced: 43.1 us -> 40.2 us
  Pallas kernels: 38.8 us -> 35.9 us
    pallas_call x1, Pallas kernels: 38.8 us -> 35.9 us  [shards(): pl.pallas_call(functools.partial(kernel, clips, parts), out_shape=jax.Sha...]
where the time goes in v4:
time: 40.9 us; the launch traced here: 40.2 us
  Pallas kernels  35.9 us (88%)
  local copies, waits for them, and re-layouts  4.23 us (10%)
    pallas_call x1, Pallas kernels, shards(): pl.pallas_call(functools.partial(kernel, clips, parts), out_shape=jax.Sha...  35.9 us
    unnamed x9, local copies, waits for them, and re-layouts  2.59 us
    transpose x1, local copies, waits for them, and re-layouts, shards(): return restored.transpose(3, 0, 1, 2)  1.64 us

profile of v4, /device:TPU:17, one launch (start us, length us, event | category | flops | bytes accessed | tf_op | source)
XLA Modules:
  0.0 40.2 jit_solution(3296778754922301130)
XLA Ops:
  0.0 0.0 copy-start
  0.0 0.0 copy-start.2
  0.0 0.0 copy-start.1
  0.0 2.0 %copy.6 = bf16[120,2,8,256]{0,3,2,1:T(8,128)(2,1)S(1)} copy(bf16[120,2,8,256]{3,2,1,0:T(8,128)(2,1)} %param.5) | data formatting | bytes 1966080 | tf_op args[0]
  2.0 0.0 copy-start.3
  2.0 0.0 copy-done
  2.0 0.0 copy-done.2
  2.0 0.0 copy-done.1
  2.0 0.6 %copy-done.3 = f32[120]{0:T(128)S(1)} copy-done((f32[120]{0:T(128)S(1)}, f32[120]{0:T(128)}, u32[]{:S(2)}) %copy-start.3) | copy-done | bytes 504
  2.6 35.9 %shard_map.55 = bf16[2,8,256,120]{3,2,1,0:T(8,128)(2,1)S(1)} custom-call(bf16[2,8,256,120]{3,2,1,0:T(8,128)(2,1)S(1)} %bitcast.3, f32[120]{0:T(128)S(1)} %copy-done.3, bf16[360,120]{1,0:T(8,128)(2,1)S(1)} %copy-done.1, bf16[120,240]{1,0:T(8,128)(2,1)S(1)} %copy-done.2, bf16[2,3,3,120,120]{4,3,2,1,0:T(8,128)(2,1)S(1)} %copy-done), custom_call_target="tpu_custom_call" | custom-call | tf_op jit(solution)/shard_map/pallas_call | solution.py:416
  38.6 1.6 %copy.7 = bf16[120,2,8,256]{3,2,1,0:T(8,128)(2,1)} copy(bf16[120,2,8,256]{0,3,2,1:T(8,128)(2,1)S(1)} %bitcast.2) | data formatting | bytes 1966080 | tf_op jit(solution)/shard_map/transpose | solution.py:449
Async XLA Ops:
  0.0 2.0 %copy-start = (bf16[2,3,3,120,120]{4,3,2,1,0:T(8,128)(2,1)S(1)}, bf16[2,3,3,120,120]{4,3,2,1,0:T(8,128)(2,1)}, u32[]{:S(2)}) copy-start(bf16[2,3,3,120,120]{4,3,2,1,0:T(8,128)(2,1)} %wconv_ref.1) | copy-start | bytes 1555204
  0.0 2.0 %copy-start.2 = (bf16[120,240]{1,0:T(8,128)(2,1)S(1)}, bf16[120,240]{1,0:T(8,128)(2,1)}, u32[]{:S(2)}) copy-start(bf16[120,240]{1,0:T(8,128)(2,1)} %wproj_ref.1) | copy-start | bytes 172804
  0.0 2.0 %copy-start.1 = (bf16[360,120]{1,0:T(8,128)(2,1)S(1)}, bf16[360,120]{1,0:T(8,128)(2,1)}, u32[]{:S(2)}) copy-start(bf16[360,120]{1,0:T(8,128)(2,1)} %wqkv_ref.1) | copy-start | bytes 259204
  2.0 0.7 %copy-start.3 = (f32[120]{0:T(128)S(1)}, f32[120]{0:T(128)}, u32[]{:S(2)}) copy-start(f32[120]{0:T(128)} %gain_ref.1) | copy-start | bytes 1444

commit v5 on v4

--- a/solution.py
+++ b/solution.py
@@ -245,12 +245,12 @@
 
     lax.fori_loop(0, windows // GROUP, self_window, 0)
 
-    wc_s[...] = jnp.zeros_like(wc_s)
     for layer in range(2):
         for r in range(3):
             for s in range(3):
-                weight = pad_rows(wconv_ref[layer, r, s].astype(F32), CP).astype(BF16)
-                wc_s[layer, s * CP : (s + 1) * CP, r * CP : r * CP + C] = weight
+                weight = pad_rows(wconv_ref[layer, r, s].astype(F32), CP).T
+                weight = pad_rows(weight, CP).astype(BF16)
+                wc_s[layer, r * CP : (r + 1) * CP, s * CP : (s + 1) * CP] = weight
     for slot, row in ((left1_s, 0), (left2_s, 0), (right1_s, width), (right2_s, width)):
         slot[:, row : row + 8] = jnp.zeros((slot.shape[0], 8, CP), F32)
 
@@ -298,7 +298,11 @@
             device_id_type=MESH,
         )
 
-    def products(field, jobs, layer, slots, start, stop):
+    def products(field, every, layer, slots, start, stop):
+        for first in range(0, len(every), 4):
+            product(field, every[first : first + 4], layer, slots, start, stop)
+
+    def product(field, jobs, layer, slots, start, stop):
         stacked = jnp.concatenate(
             [
                 jnp.concatenate([field[f, row + r, start:stop] for r in range(3)], axis=1)
@@ -306,7 +310,7 @@
             ],
             axis=0,
         )
-        part = dot_nt(stacked, wc_s[layer])
+        part = dot(stacked, wc_s[layer])
         size = stop - start
         left, middle, right = slots
         for i, (f, row) in enumerate(jobs):

time: 40.9 us -> 40.5 us (level)
  no operation moved by 1% of the time
where the time goes in v5:
time: 40.5 us; the launch traced here: 39.9 us
  Pallas kernels  35.7 us (88%)
  local copies, waits for them, and re-layouts  4.23 us (10%)
    pallas_call x1, Pallas kernels, shards(): pl.pallas_call(functools.partial(kernel, clips, parts), out_shape=jax.Sha...  35.7 us
    unnamed x9, local copies, waits for them, and re-layouts  2.59 us
    transpose x1, local copies, waits for them, and re-layouts, shards(): return restored.transpose(3, 0, 1, 2)  1.64 us

profile of v5, /device:TPU:17, one launch (start us, length us, event | category | flops | bytes accessed | tf_op | source)
XLA Modules:
  0.0 39.9 jit_solution(15840740385214509063)
XLA Ops:
  0.0 0.0 copy-start
  0.0 0.0 copy-start.2
  0.0 0.0 copy-start.1
  0.0 2.0 %copy.6 = bf16[120,2,8,256]{0,3,2,1:T(8,128)(2,1)S(1)} copy(bf16[120,2,8,256]{3,2,1,0:T(8,128)(2,1)} %param.5) | data formatting | bytes 1966080 | tf_op args[0]
  2.0 0.0 copy-start.3
  2.0 0.0 copy-done
  2.0 0.0 copy-done.2
  2.0 0.0 copy-done.1
  2.0 0.6 %copy-done.3 = f32[120]{0:T(128)S(1)} copy-done((f32[120]{0:T(128)S(1)}, f32[120]{0:T(128)}, u32[]{:S(2)}) %copy-start.3) | copy-done | bytes 504
  2.6 35.7 %shard_map.55 = bf16[2,8,256,120]{3,2,1,0:T(8,128)(2,1)S(1)} custom-call(bf16[2,8,256,120]{3,2,1,0:T(8,128)(2,1)S(1)} %bitcast.3, f32[120]{0:T(128)S(1)} %copy-done.3, bf16[360,120]{1,0:T(8,128)(2,1)S(1)} %copy-done.1, bf16[120,240]{1,0:T(8,128)(2,1)S(1)} %copy-done.2, bf16[2,3,3,120,120]{4,3,2,1,0:T(8,128)(2,1)S(1)} %copy-done), custom_call_target="tpu_custom_call" | custom-call | tf_op jit(solution)/shard_map/pallas_call | solution.py:420
  38.3 1.6 %copy.7 = bf16[120,2,8,256]{3,2,1,0:T(8,128)(2,1)} copy(bf16[120,2,8,256]{0,3,2,1:T(8,128)(2,1)S(1)} %bitcast.2) | data formatting | bytes 1966080 | tf_op jit(solution)/shard_map/transpose | solution.py:453
Async XLA Ops:
  0.0 2.0 %copy-start = (bf16[2,3,3,120,120]{4,3,2,1,0:T(8,128)(2,1)S(1)}, bf16[2,3,3,120,120]{4,3,2,1,0:T(8,128)(2,1)}, u32[]{:S(2)}) copy-start(bf16[2,3,3,120,120]{4,3,2,1,0:T(8,128)(2,1)} %wconv_ref.1) | copy-start | bytes 1555204
  0.0 2.0 %copy-start.2 = (bf16[120,240]{1,0:T(8,128)(2,1)S(1)}, bf16[120,240]{1,0:T(8,128)(2,1)}, u32[]{:S(2)}) copy-start(bf16[120,240]{1,0:T(8,128)(2,1)} %wproj_ref.1) | copy-start | bytes 172804
  0.0 2.0 %copy-start.1 = (bf16[360,120]{1,0:T(8,128)(2,1)S(1)}, bf16[360,120]{1,0:T(8,128)(2,1)}, u32[]{:S(2)}) copy-start(bf16[360,120]{1,0:T(8,128)(2,1)} %wqkv_ref.1) | copy-start | bytes 259204
  2.0 0.7 %copy-start.3 = (f32[120]{0:T(128)S(1)}, f32[120]{0:T(128)}, u32[]{:S(2)}) copy-start(f32[120]{0:T(128)} %gain_ref.1) | copy-start | bytes 1444

commit v6 on v5

--- a/solution.py
+++ b/solution.py
@@ -19,9 +19,9 @@
 CUTS = (8, 8, 8, 4, 4)
 GROUP = 8
 LAG = 16
-LAG1 = 4
-LAG2 = 6
-LAG3 = 8
+LAG1 = 6
+LAG2 = 8
+LAG3 = 10
 MESH = pl.DeviceIdType.MESH
 F32 = jnp.float32
 BF16 = jnp.bfloat16
@@ -393,11 +393,12 @@
     conv_inside(done, width)
     rows1 = (0, 1, own_rows, own_rows + 1)
     rows2 = (0, 1, own_rows - 2, own_rows - 1)
-    for k in range(len(spans) - 1):
-        wait_halo(k)
-    conv_rows(rows1, rows2, 0, spans[-1][0] * WIN)
-    wait_halo(len(spans) - 1)
-    conv_rows(rows1, rows2, spans[-1][0] * WIN, width)
+    done = 0
+    for group in ((0,), (1, 2), (3, 4)):
+        for k in group:
+            wait_halo(k)
+        conv_rows(rows1, rows2, done, spans[group[-1]][1] * WIN)
+        done = spans[group[-1]][1] * WIN
 
     for k in range(len(spans)):
         for copy, low, high in ((clip_copy, has_next, has_prev), (halo_copy, has_up, has_down)):

time: 40.5 us -> 40.6 us (level)
  no operation moved by 1% of the time
where the time goes in v6:
time: 40.6 us; the launch traced here: 40.2 us
  Pallas kernels  35.9 us (88%)
  local copies, waits for them, and re-layouts  4.23 us (10%)
    pallas_call x1, Pallas kernels, shards(): pl.pallas_call(functools.partial(kernel, clips, parts), out_shape=jax.Sha...  35.9 us
    unnamed x9, local copies, waits for them, and re-layouts  2.59 us
    transpose x1, local copies, waits for them, and re-layouts, shards(): return restored.transpose(3, 0, 1, 2)  1.64 us

profile of v6, /device:TPU:17, one launch (start us, length us, event | category | flops | bytes accessed | tf_op | source)
XLA Modules:
  0.0 40.2 jit_solution(8608904562143166713)
XLA Ops:
  0.0 0.0 copy-start
  0.0 0.0 copy-start.2
  0.0 0.0 copy-start.1
  0.0 2.0 %copy.6 = bf16[120,2,8,256]{0,3,2,1:T(8,128)(2,1)S(1)} copy(bf16[120,2,8,256]{3,2,1,0:T(8,128)(2,1)} %param.5) | data formatting | bytes 1966080 | tf_op args[0]
  2.0 0.0 copy-start.3
  2.0 0.0 copy-done
  2.0 0.0 copy-done.2
  2.0 0.0 copy-done.1
  2.0 0.6 %copy-done.3 = f32[120]{0:T(128)S(1)} copy-done((f32[120]{0:T(128)S(1)}, f32[120]{0:T(128)}, u32[]{:S(2)}) %copy-start.3) | copy-done | bytes 504
  2.6 35.9 %shard_map.55 = bf16[2,8,256,120]{3,2,1,0:T(8,128)(2,1)S(1)} custom-call(bf16[2,8,256,120]{3,2,1,0:T(8,128)(2,1)S(1)} %bitcast.3, f32[120]{0:T(128)S(1)} %copy-done.3, bf16[360,120]{1,0:T(8,128)(2,1)S(1)} %copy-done.1, bf16[120,240]{1,0:T(8,128)(2,1)S(1)} %copy-done.2, bf16[2,3,3,120,120]{4,3,2,1,0:T(8,128)(2,1)S(1)} %copy-done), custom_call_target="tpu_custom_call" | custom-call | tf_op jit(solution)/shard_map/pallas_call | solution.py:421
  38.6 1.6 %copy.7 = bf16[120,2,8,256]{3,2,1,0:T(8,128)(2,1)} copy(bf16[120,2,8,256]{0,3,2,1:T(8,128)(2,1)S(1)} %bitcast.2) | data formatting | bytes 1966080 | tf_op jit(solution)/shard_map/transpose | solution.py:454
Async XLA Ops:
  0.0 2.0 %copy-start = (bf16[2,3,3,120,120]{4,3,2,1,0:T(8,128)(2,1)S(1)}, bf16[2,3,3,120,120]{4,3,2,1,0:T(8,128)(2,1)}, u32[]{:S(2)}) copy-start(bf16[2,3,3,120,120]{4,3,2,1,0:T(8,128)(2,1)} %wconv_ref.1) | copy-start | bytes 1555204
  0.0 2.0 %copy-start.2 = (bf16[120,240]{1,0:T(8,128)(2,1)S(1)}, bf16[120,240]{1,0:T(8,128)(2,1)}, u32[]{:S(2)}) copy-start(bf16[120,240]{1,0:T(8,128)(2,1)} %wproj_ref.1) | copy-start | bytes 172804
  0.0 2.0 %copy-start.1 = (bf16[360,120]{1,0:T(8,128)(2,1)S(1)}, bf16[360,120]{1,0:T(8,128)(2,1)}, u32[]{:S(2)}) copy-start(bf16[360,120]{1,0:T(8,128)(2,1)} %wqkv_ref.1) | copy-start | bytes 259204
  2.0 0.7 %copy-start.3 = (f32[120]{0:T(128)S(1)}, f32[120]{0:T(128)}, u32[]{:S(2)}) copy-start(f32[120]{0:T(128)} %gain_ref.1) | copy-start | bytes 1444
